TPU v7x, 32 devices: a whole 2x2x4 slice. The times are simulated.
32 devices in a mesh: depth: 8 (over z, x), dp: 4 (over y, core).
Axes of the slice: x: 2, y: 2, z: 4, core: 2. Of those that a mesh axis runs over, the one named last changes fastest.
Arguments:
- cpoints: float32 [8, 4, 64, 256], P('depth', 'dp'), may hold values from -6 to 6, as said below
- weights: bfloat16 [32, 64, 576], P('depth'), may hold values from -0.75 to 0.75
- coarse_gain: float32 [8, 64], P('depth'), may hold values from 0.04 to 1
- cotangent: float32 [8, 4, 64, 256], P('depth', 'dp'), may hold values from -0.6 to 0.6
Outputs:
- corrected: float32 [8, 4, 64, 256], P('depth', 'dp')
- grad_cpoints: float32 [8, 4, 64, 256], P('depth', 'dp')
- grad_weights: float32 [32, 64, 576], P('depth')
Inputs may be any that keep to these rules, and one draw needn't show every extreme that they name: cpoints[0] holds the network input; cpoints[d] the current guess of the state entering block d.
All inputs are finite; a program needn't handle non-finite values.
Results may differ from a plain program's by a relative error of at most 0.0041.
Values sent between devices are 32-bit elements; how exact they have to be, the bound alone decides.
A program may use at most 64 MiB of HBM per device.

v0:
```python
import jax
import jax.numpy as jnp
from jax import lax
from jax.sharding import PartitionSpec as P

WID = 16


TAP_OFFSETS = [(-1, -1), (-1, 0), (-1, 1), (0, -1), (0, 0), (0, 1), (1, -1), (1, 0), (1, 1)]


def prefix(part, axis, combine, identity, reverse):
    count = lax.axis_size(axis)
    place = lax.axis_index(axis)
    ahead = count - 1 - place if reverse else place
    gathered = jax.tree.map(lambda a: lax.all_gather(a, axis), part)
    state = jax.tree.map(lambda a, e: jnp.zeros_like(a) + jnp.asarray(e, a.dtype), part, identity)

    def one(hop, state):
        source = count - 1 - hop if reverse else hop
        return combine(
            state, jax.tree.map(lambda a: lax.dynamic_index_in_dim(a, source, 0, False), gathered)
        )

    return lax.fori_loop(0, ahead, one, state)


def passed_along(block, axis, distance):
    devices = range(lax.axis_size(axis))
    route = [(i - distance, i) for i in devices if i - distance in devices]
    return lax.ppermute(block, axis, route)


def shift_pixels(values, shift_down, shift_right, row_width):
    pixel_count = values.shape[-1]
    offset = shift_down * row_width + shift_right
    padded = jnp.pad(values, [(0, 0)] * (values.ndim - 1) + [(row_width + 1, row_width + 1)])
    shifted = lax.slice_in_dim(
        padded, row_width + 1 + offset, row_width + 1 + offset + pixel_count, axis=values.ndim - 1
    )
    column = jnp.arange(pixel_count) % row_width + shift_right
    inside = (column >= 0) & (column < row_width)
    return jnp.where(inside, shifted, jnp.zeros_like(shifted))


def unfold(values, row_width):
    return jnp.concatenate([shift_pixels(values, a, b, row_width) for a, b in TAP_OFFSETS], axis=1)


def fold_taps(tap_grads, row_width):
    channels = tap_grads.shape[1] // 9
    accumulated = jnp.zeros((tap_grads.shape[0], channels, tap_grads.shape[2]), jnp.float32)
    for tap_index, (a, b) in enumerate(TAP_OFFSETS):
        piece = tap_grads[:, tap_index * channels : (tap_index + 1) * channels]
        accumulated = accumulated + shift_pixels(piece, -a, -b, row_width)
    return accumulated


def run_block(current, block_weights, step_size):
    inputs_kept = []
    for layer in range(block_weights.shape[0]):
        inputs_kept.append(current)
        squashed = jnp.tanh(current)
        patches = unfold(squashed.astype(jnp.bfloat16), WID)
        mixed = jnp.einsum(
            "ok,bkp->bop", block_weights[layer], patches, preferred_element_type=jnp.float32
        )
        current = current + step_size * mixed
    return (current, inputs_kept)


def back_block(inputs_kept, block_weights, upstream, step_size):
    layer_count = block_weights.shape[0]
    layer_grads = [None] * layer_count
    for layer in reversed(range(layer_count)):
        squashed = jnp.tanh(inputs_kept[layer])
        patches = unfold(squashed.astype(jnp.bfloat16), WID)
        scaled = (step_size * upstream).astype(jnp.bfloat16)
        layer_grads[layer] = jnp.einsum(
            "bop,bkp->ok", scaled, patches, preferred_element_type=jnp.float32
        )
        spread = jnp.einsum(
            "ok,bop->bkp", block_weights[layer], scaled, preferred_element_type=jnp.float32
        )
        upstream = upstream + (1.0 - squashed * squashed) * fold_taps(spread, WID)
    return (upstream, jnp.stack(layer_grads))


def compose_maps(earlier, later):
    return (later[0] * earlier[0], later[0][None, :, None] * earlier[1] + later[1])


def adjoint_carry(rate_vec, incoming):
    identity_maps = (jnp.ones_like(rate_vec), jnp.zeros_like(incoming))
    _, passed_in = prefix(
        (rate_vec, rate_vec[None, :, None] * incoming), "depth", compose_maps, identity_maps, True
    )
    return passed_in


def body(cpoints, weights, coarse_gain, cotangent):
    step_size = 1.0 / (weights.shape[0] * lax.axis_size("depth"))
    own_state = cpoints[0]
    rate_vec = coarse_gain[0]
    cot_here = cotangent[0]
    leading = lax.axis_index("depth") == 0
    relaxed, own_kept = run_block(own_state, weights, step_size)
    arriving = passed_along(relaxed, "depth", 1)
    start_state = jnp.where(leading, own_state, arriving)
    propagated, start_kept = run_block(start_state, weights, step_size)
    gained_start = rate_vec[None, :, None] * start_state
    offset = propagated - jnp.where(leading, jnp.zeros_like(gained_start), gained_start)
    identity_maps = (jnp.ones_like(rate_vec), jnp.zeros_like(offset))
    _, previous_out = prefix((rate_vec, offset), "depth", compose_maps, identity_maps, False)
    corrected = rate_vec[None, :, None] * previous_out + offset
    passed_in = adjoint_carry(rate_vec, cot_here)
    adjoint_here = cot_here + passed_in
    back_start, start_grads = back_block(start_kept, weights, adjoint_here, step_size)
    arriving_bar = passed_along(back_start, "depth", -1)
    relaxed_bar = arriving_bar - passed_in
    back_own, own_grads = back_block(own_kept, weights, relaxed_bar, step_size)
    grad_cpoints = jnp.where(leading, back_own + back_start, back_own)
    grad_weights = lax.psum(start_grads + own_grads, "dp")
    return (corrected[None], grad_cpoints[None], grad_weights)


def solution(mesh):
    placed = (
        P("depth", "dp", None, None),
        P("depth", None, None),
        P("depth", None),
        P("depth", "dp", None, None),
    )
    return jax.shard_map(
        body,
        mesh=mesh,
        in_specs=placed,
        out_specs=(
            P("depth", "dp", None, None),
            P("depth", "dp", None, None),
            P("depth", None, None),
        ),
        check_vma=False,
    )
```

profile of v0, /device:TPU:0, one launch (start us, length us, event | category | flops | bytes accessed | tf_op | source)
XLA Modules:
  0.0 166.7 jit_solution(7410251890354514529)
XLA Ops:
  7.2 0.9 fusion.193
  8.4 0.1 constant_dynamic-update-slice_fusion.6
  8.6 0.1 constant_dynamic-update-slice_fusion.3
  8.9 0.3 copy-done
  9.1 0.2 tanh_convert_fusion.6
  9.5 0.1 constant_dynamic-update-slice_fusion.15
  9.7 0.1 constant_dynamic-update-slice_fusion.12
  10.0 0.2 tanh_convert_fusion.5
  10.4 0.1 constant_dynamic-update-slice_fusion.24
  10.6 0.1 constant_dynamic-update-slice_fusion.21
  11.0 0.2 tanh_convert_fusion.4
  11.3 0.1 constant_dynamic-update-slice_fusion.33
  11.9 0.2 fusion.11
  12.1 4.8 %collective-permute-start = (f32[1,64,256]{2,1,0:T(8,128)S(1)}, f32[1,64,256]{2,1,0:T(8,128)S(1)}, u32[]{:S(2)}, u32[]{:S(2)}) collective-permute-start(f32[1,64,256]{2,1,0:T(8,128)S(1)} %fusion.11), channel_id=1, source_target_pairs={{0,4},{4,8},{8,12},{12,16},{16,20},{20,24},{24,28},{1,5},{5,9},{9,... | collective-permute-start | bytes 196616 | tf_op jit(solution)/shard_map/ppermute | solution.py:31
  16.9 0.6 copy-done.11
  17.6 18.6 %all-gather.1 = f32[8,1,64]{2,1,0:T(1,128)S(1)} all-gather(f32[1,1,64]{2,1,0:T(1,128)S(1)} %bitcast.278), channel_id=1, replica_groups=mesh['depth'=8,'dp'=4] {'depth'}, dimensions={0}, use_global_device_ids=true | all-gather | bytes 2304 | tf_op jit(solution)/shard_map/all_gather | solution.py:16
  36.2 31.5 %all_gather.17 = f32[8,1,64,256]{3,2,1,0:T(8,128)S(1)} all-gather(f32[1,1,64,256]{3,2,1,0:T(8,128)S(1)} %broadcast_multiply_fusion), channel_id=1, replica_groups=mesh['depth'=8,'dp'=4] {'depth'}, dimensions={0}, use_global_device_ids=true | all-gather | bytes 589824 | tf_op jit(solution)/shard_map/all_gather | solution.py:16
  67.7 0.8 while.27
  67.7 0.1 bitcast_add_fusion.6
  67.9 0.1 bitcast_add_fusion.6
  68.0 0.1 bitcast_add_fusion.6
  68.1 0.1 bitcast_add_fusion.6
  68.2 0.1 bitcast_add_fusion.6
  68.4 0.1 bitcast_add_fusion.6
  68.5 0.1 bitcast_add_fusion.6
  68.6 0.6 copy-done.12
  69.2 0.3 convolution_bitcast_fusion.7
  69.5 0.3 copy-done.9
  70.6 0.2 tanh_convert_fusion.2
  71.5 0.2 tanh_convert_fusion.1
  72.4 0.2 fusion.58
  72.6 0.2 convolution_bitcast_fusion.13
  72.8 0.3 convolution_bitcast_fusion.6
  73.2 0.2 fusion.76
  73.4 0.9 convolution_bitcast_fusion.14
  74.2 0.3 convolution_bitcast_fusion.5
  74.6 0.2 fusion.94
  74.8 0.9 convolution_bitcast_fusion.15
  75.7 0.3 convolution_bitcast_fusion.4
  76.7 0.2 select_subtract_fusion
  76.8 31.5 %all-gather = f32[8,64,256]{2,1,0:T(8,128)S(1)} all-gather(f32[1,64,256]{2,1,0:T(8,128)S(1)} %select_subtract_fusion), channel_id=2, replica_groups=mesh['depth'=8,'dp'=4] {'depth'}, dimensions={0}, use_global_device_ids=true | all-gather | bytes 589824 | tf_op jit(solution)/shard_map/all_gather | solution.py:16
  108.4 0.7 add_bitcast_fusion
  109.1 0.2 fusion.112
  109.3 1.3 collective-permute-start.1
  110.6 0.2 convolution_bitcast_fusion.12
  110.9 4.6 %collective-permute-done.1 = f32[1,64,256]{2,1,0:T(8,128)S(1)} collective-permute-done((f32[1,64,256]{2,1,0:T(8,128)S(1)}, f32[1,64,256]{2,1,0:T(8,128)S(1)}, u32[]{:S(2)}, u32[]{:S(2)}) %collective-permute-start.1) | collective-permute-done | bytes 65568 | tf_op jit(solution)/shard_map/ppermute | solution.py:31
  115.5 0.2 convolution_bitcast_fusion.8
  115.7 0.3 convolution_bitcast_fusion.3
  116.1 0.8 copy-done.8
  116.9 0.2 fusion.130
  117.1 0.2 convolution_bitcast_fusion.9
  117.3 0.3 convolution_bitcast_fusion.2
  117.6 0.8 copy-done.6
  118.4 0.2 fusion.148
  118.6 0.2 convolution_bitcast_fusion.10
  118.8 0.3 convolution_bitcast_fusion.1
  119.2 0.2 fusion.166
  119.4 0.2 convolution_bitcast_fusion.11
  119.6 0.3 convolution_bitcast_fusion
  119.9 0.6 copy-done.2
  120.6 0.9 maximum_add_fusion
  121.6 0.8 fusion.192
  122.5 35.4 %all-reduce.74.cloned.1.call-done = f32[4,64,576]{2,1,0:T(8,128)} async-done(((f32[4,64,576]{2,1,0:T(8,128)}), f32[4,64,576]{2,1,0:T(8,128)}) %all-reduce.74.cloned.1.call-update) | async-done | bytes 589840 | tf_op jit(solution)/shard_map/psum | solution.py:123
  157.9 2.0 %copy.86 = f32[4,64,576]{2,1,0:T(8,128)} copy(f32[4,64,576]{2,1,0:T(8,128)} %all-reduce.74.cloned.1.call-done) | data formatting | bytes 1179648
  (111 shorter events, 5.5 us)
Async XLA Ops:
  7.2 150.7 %all-reduce.74.cloned.1.call-start = ((), (), s32[]{:S(2)}) async-start(), calls=%async_computation | async-start | bytes 1310720 | tf_op jit(solution)/shard_map/psum | solution.py:123
  7.2 1.3 copy-start.1
  8.2 1.0 copy-start
  10.2 0.7 copy-start.5
  11.2 0.7 copy-start.7
  11.9 24.3 %copy-start.4 = (f32[1,1,64,256]{3,2,1,0:T(8,128)S(1)}, f32[1,1,64,256]{3,2,1,0:T(8,128)}, u32[]{:S(2)}) copy-start(f32[1,1,64,256]{3,2,1,0:T(8,128)} %param.11) | copy-start | bytes 196612
  12.1 57.8 %collective-permute-start = (f32[1,64,256]{2,1,0:T(8,128)S(1)}, f32[1,64,256]{2,1,0:T(8,128)S(1)}, u32[]{:S(2)}, u32[]{:S(2)}) collective-permute-start(f32[1,64,256]{2,1,0:T(8,128)S(1)} %fusion.11), channel_id=1, source_target_pairs={{0,4},{4,8},{8,12},{12,16},{16,20},{20,24},{24,28},{1,5},{5,9},{9,... | collective-permute-start | bytes 196616 | tf_op jit(solution)/shard_map/ppermute | solution.py:31
  16.9 0.7 copy-start.11
  68.6 0.6 copy-start.12
  69.2 0.6 copy-start.9
  109.1 1.5 copy-start.10
  109.3 6.2 %collective-permute-start.1 = (f32[1,64,256]{2,1,0:T(8,128)S(1)}, f32[1,64,256]{2,1,0:T(8,128)S(1)}, u32[]{:S(2)}, u32[]{:S(2)}) collective-permute-start(f32[1,64,256]{2,1,0:T(8,128)S(1)} %fusion.112), channel_id=1, source_target_pairs={{4,0},{8,4},{12,8},{16,12},{20,16},{24,20},{28,24},{5,1},{9,5},{13... | collective-permute-start | bytes 196616 | tf_op jit(solution)/shard_map/ppermute | solution.py:31
  116.0 0.8 copy-start.8
  117.6 0.8 copy-start.6
  119.6 0.9 copy-start.2
  119.6 1.0 copy-start.3
Sparse Core Ops, SparseCore 0:
  121.7 36.1 all-reduce.73
where the time goes:
time: 167 us
  blocking collectives  81.6 us (49%)
  waiting for transfers between devices  40.1 us (24%)
  between operations  14.7 us (9%)
  other arithmetic  10.7 us (6%)
  matrix products  6.87 us (4%)
  local copies, waits for them, and re-layouts  6.44 us (4%)
  starting transfers between devices  6.17 us (4%)
    all_gather x3, blocking collectives, prefix(): gathered = jax.tree.map(lambda a: lax.all_gather(a, axis), part)  81.6 us
    psum x1, waiting for transfers between devices, body(): grad_weights = lax.psum(start_grads + own_grads, 'dp')  35.4 us
    ppermute x2, starting transfers between devices, passed_along(): return lax.ppermute(block, axis, route)  6.14 us
    unnamed x27, local copies, waits for them, and re-layouts  6.06 us
    unnamed x64, other arithmetic  4.68 us
    ppermute x2, waiting for transfers between devices, passed_along(): return lax.ppermute(block, axis, route)  4.65 us
  transfers between devices with their start and end apart: 3, of which 2 were waited for; matrix products, arithmetic and copies ran while one was open for 1% of the time, Pallas kernels for 0%

commit v1 on v0

v1 whole, which is shorter than its diff:
```python
import functools

import jax
import jax.numpy as jnp
from jax import lax
from jax.experimental import pallas as pl
from jax.experimental.pallas import tpu as pltpu
from jax.sharding import PartitionSpec as P

MESH = pl.DeviceIdType.MESH
WID = 16
TAP_OFFSETS = [(-1, -1), (-1, 0), (-1, 1), (0, -1), (0, 0), (0, 1), (1, -1), (1, 0), (1, 1)]


def kernel(
    depth,
    dp,
    cp_ref,
    w_ref,
    gain_ref,
    cot_ref,
    corr_ref,
    gcp_ref,
    gw_ref,
    patches,
    slopes,
    back_patches,
    turned,
    start_grads,
    relaxed_buf,
    start_buf,
    back_buf,
    bar_buf,
    passed_buf,
    gains,
    gains_in,
    adj_out,
    adj_in,
    fwd,
    fwd_in,
    sum_a,
    sum_b,
    part_a,
    part_b,
    gain_send,
    gain_recv,
    adj_send,
    adj_recv,
    fwd_send,
    fwd_recv,
    edge_send,
    edge_recv,
    a_send,
    a_recv,
    b_send,
    b_recv,
    c_send,
    c_recv,
):
    layers, channels, width = w_ref.shape
    pixels = cp_ref.shape[-1]
    half = channels // 2
    step_size = 1.0 / (layers * depth)
    hops = []
    while 2 ** len(hops) < depth:
        hops.append(2 ** len(hops))
    rounds = len(hops)
    me = lax.axis_index("depth")
    lane = lax.axis_index("dp")
    side = lane % 2
    sibling = lane + 1 - 2 * side
    across = (lane + 2) % dp

    barrier = pltpu.get_barrier_semaphore()
    count = 2
    for mate in (sibling, across):
        pl.semaphore_signal(barrier, inc=1, device_id={"dp": mate}, device_id_type=MESH)
    for hop in hops:
        ahead, behind = me + hop < depth, me >= hop
        count = count + jnp.where(ahead, 1, 0) + jnp.where(behind, 1, 0)

        @pl.when(ahead)
        def _():
            pl.semaphore_signal(barrier, inc=1, device_id={"depth": me + hop}, device_id_type=MESH)

        @pl.when(behind)
        def _():
            pl.semaphore_signal(barrier, inc=1, device_id={"depth": me - hop}, device_id_type=MESH)

    pixel = lax.broadcasted_iota(jnp.int32, (1, pixels), 1)
    row, column = pixel // WID, pixel % WID
    masks = []
    for a, b in TAP_OFFSETS:
        ok = (row + a >= 0) & (row + a < pixels // WID) & (column + b >= 0) & (column + b < WID)
        masks.append(jnp.broadcast_to(ok, (channels, pixels)))

    def unfold(values, ref):
        for t, (a, b) in enumerate(TAP_OFFSETS):
            off = a * WID + b
            moved = values
            if off:
                moved = jnp.where(masks[t], pltpu.roll(values, (-off) % pixels, 1), 0.0)
            ref[t * channels : (t + 1) * channels, :] = moved.astype(jnp.bfloat16)

    def forward_layer(u, layer, which):
        squashed = jnp.tanh(u)
        slopes[which, layer] = 1.0 - squashed * squashed
        unfold(squashed, patches.at[which, layer])
        mixed = jnp.dot(
            w_ref[layer], patches[which, layer], preferred_element_type=jnp.float32
        )
        return u + step_size * mixed

    def backward_layer(g, layer, which):
        scaled = step_size * g
        rounded = scaled.astype(jnp.bfloat16)
        unfold(rounded.astype(jnp.float32), back_patches)
        grads = lax.dot_general(
            rounded,
            patches[which, layer],
            (((1,), (1,)), ((), ())),
            preferred_element_type=jnp.float32,
        )
        spread = jnp.dot(turned[layer], back_patches[...], preferred_element_type=jnp.float32)
        return g + slopes[which, layer] * spread, grads

    def along(src, dst, send, recv, target):
        return pltpu.make_async_remote_copy(
            src_ref=src,
            dst_ref=dst,
            send_sem=send,
            recv_sem=recv,
            device_id=target,
            device_id_type=MESH,
        )

    def gain_copy(r):
        return along(
            gains.at[r], gains_in.at[r], gain_send.at[r], gain_recv.at[r], {"depth": me + hops[r]}
        )

    def adj_copy(r):
        return along(
            adj_out.at[r], adj_in.at[r], adj_send.at[r], adj_recv.at[r], {"depth": me - hops[r]}
        )

    def fwd_copy(r):
        return along(
            fwd.at[r], fwd_in.at[r], fwd_send.at[r], fwd_recv.at[r], {"depth": me + hops[r]}
        )

    def relaxed_copy():
        return along(relaxed_buf, start_buf, edge_send.at[0], edge_recv.at[0], {"depth": me + 1})

    def back_copy():
        return along(back_buf, bar_buf, edge_send.at[1], edge_recv.at[1], {"depth": me - 1})

    eye = lax.broadcasted_iota(jnp.int32, (channels, channels), 0) == lax.broadcasted_iota(
        jnp.int32, (channels, channels), 1
    )

    def gain_column(r):
        line = jnp.broadcast_to(gains[r, 0:1, 0:channels], (channels, channels))
        return jnp.sum(jnp.where(eye, line, 0.0), axis=1, keepdims=True)

    def start_adj(r):
        @pl.when(me >= hops[r])
        def _():
            adj_out[r] = gain_column(r) * (cot_ref[0, 0] + passed_buf[...])
            adj_copy(r).start()

    def take_gain(r):
        @pl.when(me >= hops[r])
        def _():
            gain_copy(r).wait_recv()
            gains[r + 1] = gains[r] * gains_in[r]

        @pl.when(me < hops[r])
        def _():
            gains[r + 1] = gains[r]

    def start_gain(r):
        @pl.when(me + hops[r] < depth)
        def _():
            gain_copy(r).start()

    def take_adj(r):
        @pl.when(me + hops[r] < depth)
        def _():
            adj_copy(r).wait_recv()
            passed_buf[...] = passed_buf[...] + adj_in[r]

    def start_fwd(r):
        @pl.when(me + hops[r] < depth)
        def _():
            fwd_copy(r).start()

    def take_fwd(r):
        @pl.when(me >= hops[r])
        def _():
            fwd_copy(r).wait_recv()
            fwd[r + 1] = fwd[r] + gain_column(r) * fwd_in[r]

        @pl.when(me < hops[r])
        def _():
            fwd[r + 1] = fwd[r]

    gains[0] = jnp.zeros_like(gains[0])
    gains[0, 0:1, 0:channels] = gain_ref[...]
    passed_buf[...] = jnp.zeros_like(passed_buf)
    own = cp_ref[0, 0]
    u = forward_layer(own, 0, 0)
    pl.semaphore_wait(barrier, count)
    start_adj(0)
    if rounds > 1:
        start_gain(0)
    for layer in range(1, layers):
        u = forward_layer(u, layer, 0)
    relaxed_buf[...] = u

    @pl.when(me + 1 < depth)
    def _():
        relaxed_copy().start()

    for r in range(rounds - 1):
        take_gain(r)
        if r + 1 < rounds - 1:
            start_gain(r + 1)
        take_adj(r)
        start_adj(r + 1)

    one = jnp.where(eye, 1.0, 0.0).astype(jnp.bfloat16)
    for layer in range(layers):
        pieces = []
        for t in reversed(range(len(TAP_OFFSETS))):
            block = w_ref[layer, :, t * channels : (t + 1) * channels]
            pieces.append(
                lax.dot_general(
                    one, block, (((1,), (1,)), ((), ())), preferred_element_type=jnp.float32
                ).astype(jnp.bfloat16)
            )
        turned[layer] = jnp.concatenate(pieces, axis=1)

    @pl.when(me > 0)
    def _():
        relaxed_back = along(
            relaxed_buf, start_buf, edge_send.at[0], edge_recv.at[0], {"depth": me - 1}
        )
        relaxed_back.wait_recv()

    @pl.when(me == 0)
    def _():
        start_buf[...] = own

    u = start_buf[...]
    for layer in range(layers):
        u = forward_layer(u, layer, 1)
    fwd[0] = u - jnp.where(me == 0, 0.0, 1.0) * gain_column(0) * start_buf[...]
    start_fwd(0)
    take_adj(rounds - 1)

    g = cot_ref[0, 0] + passed_buf[...]
    for position, layer in enumerate(reversed(range(layers))):
        g, grads = backward_layer(g, layer, 1)
        start_grads[layer] = grads
    back_buf[...] = g

    @pl.when(me > 0)
    def _():
        back_copy().start()

    for r in range(rounds):
        take_fwd(r)
        if r + 1 < rounds:
            start_fwd(r + 1)
    corr_ref[0, 0] = fwd[rounds]

    @pl.when(me + 1 < depth)
    def _():
        back_copy().wait_recv()

    @pl.when(me + 1 == depth)
    def _():
        bar_buf[...] = jnp.zeros_like(bar_buf)

    g = bar_buf[...] - passed_buf[...]

    mine = pl.ds(pl.multiple_of(side * half, half), half)
    other = pl.ds(pl.multiple_of((1 - side) * half, half), half)

    def a_copy(layer):
        return along(
            start_grads.at[layer, other],
            part_a.at[layer],
            a_send.at[layer],
            a_recv.at[layer],
            {"dp": sibling},
        )

    def b_copy(layer):
        return along(
            sum_a.at[layer], part_b.at[layer], b_send.at[layer], b_recv.at[layer], {"dp": across}
        )

    def c_copy(layer):
        return along(
            sum_b.at[layer],
            gw_ref.at[layer, mine],
            c_send.at[layer],
            c_recv.at[layer],
            {"dp": sibling},
        )

    def middle(layer):
        a_copy(layer).wait_recv()
        sum_a[layer] = start_grads[layer, mine, :] + part_a[layer]
        b_copy(layer).start()

    def last(layer):
        b_copy(layer).wait_recv()
        sum_b[layer] = sum_a[layer] + part_b[layer]
        c_copy(layer).start()
        gw_ref[layer, mine, :] = sum_b[layer]

    for layer in reversed(range(layers)):
        g, grads = backward_layer(g, layer, 0)
        start_grads[layer] = start_grads[layer] + grads
        a_copy(layer).start()
        if layer + 1 < layers:
            middle(layer + 1)
    gcp_ref[0, 0] = g + jnp.where(me == 0, 1.0, 0.0) * back_buf[...]
    middle(0)
    for layer in reversed(range(layers)):
        last(layer)
    for layer in reversed(range(layers)):
        c_copy(layer).wait_recv()
        a_copy(layer).wait_send()
        b_copy(layer).wait_send()
        c_copy(layer).wait_send()

    for r in range(rounds):
        if r + 1 < rounds:

            @pl.when(me + hops[r] < depth)
            def _():
                gain_copy(r).wait_send()

        @pl.when(me >= hops[r])
        def _():
            adj_copy(r).wait_send()

        @pl.when(me + hops[r] < depth)
        def _():
            fwd_copy(r).wait_send()

    @pl.when(me + 1 < depth)
    def _():
        relaxed_copy().wait_send()

    @pl.when(me > 0)
    def _():
        back_copy().wait_send()


def solution(mesh):
    depth, dp = mesh.shape["depth"], mesh.shape["dp"]
    rounds = max(1, (depth - 1).bit_length())

    def step(cpoints, weights, coarse_gain, cotangent):
        layers, channels, width = weights.shape
        pixels = cpoints.shape[-1]
        state = (channels, pixels)
        half = (layers, channels // 2, width)
        f32, bf16 = jnp.float32, jnp.bfloat16
        dma = pltpu.SemaphoreType.DMA
        vmem = pl.BlockSpec(memory_space=pltpu.VMEM)
        return pl.pallas_call(
            functools.partial(kernel, depth, dp),
            out_shape=(
                jax.ShapeDtypeStruct(cpoints.shape, f32),
                jax.ShapeDtypeStruct(cpoints.shape, f32),
                jax.ShapeDtypeStruct(weights.shape, f32),
            ),
            in_specs=[vmem] * 4,
            out_specs=(vmem,) * 3,
            scratch_shapes=[
                pltpu.VMEM((2, layers, width, pixels), bf16),
                pltpu.VMEM((2, layers) + state, f32),
                pltpu.VMEM((width, pixels), bf16),
                pltpu.VMEM((layers, channels, width), bf16),
                pltpu.VMEM((layers, channels, width), f32),
                pltpu.VMEM(state, f32),
                pltpu.VMEM(state, f32),
                pltpu.VMEM(state, f32),
                pltpu.VMEM(state, f32),
                pltpu.VMEM(state, f32),
                pltpu.VMEM((rounds, 8, 128), f32),
                pltpu.VMEM((rounds, 8, 128), f32),
                pltpu.VMEM((rounds,) + state, f32),
                pltpu.VMEM((rounds,) + state, f32),
                pltpu.VMEM((rounds + 1,) + state, f32),
                pltpu.VMEM((rounds,) + state, f32),
                pltpu.VMEM(half, f32),
                pltpu.VMEM(half, f32),
                pltpu.VMEM(half, f32),
                pltpu.VMEM(half, f32),
                dma((rounds,)),
                dma((rounds,)),
                dma((rounds,)),
                dma((rounds,)),
                dma((rounds,)),
                dma((rounds,)),
                dma((2,)),
                dma((2,)),
                dma((layers,)),
                dma((layers,)),
                dma((layers,)),
                dma((layers,)),
                dma((layers,)),
                dma((layers,)),
            ],
            compiler_params=pltpu.CompilerParams(
                collective_id=0, has_side_effects=True, vmem_limit_bytes=40 * 1024 * 1024
            ),
        )(cpoints, weights, coarse_gain, cotangent)

    states = P("depth", "dp", None, None)
    blocks = P("depth", None, None)
    return jax.shard_map(
        step,
        mesh=mesh,
        in_specs=(states, blocks, P("depth", None), states),
        out_specs=(states, states, blocks),
        check_vma=False,
    )
```

time: 167 us -> 40.4 us (0.24)
  the two profiles are of different devices: /device:TPU:0 before, /device:TPU:27 now
where the time goes in v1:
time: 40.4 us; the launch traced here: 40.1 us
  Pallas kernels  34.1 us (84%)
  local copies, waits for them, and re-layouts  5.4 us (13%)
  between operations  0.65 us (2%)
    pallas_call x1, Pallas kernels, step(): pl.pallas_call(functools.partial(kernel, depth, dp), out_shape=(jax.Shape...  34.1 us
    unnamed x11, local copies, waits for them, and re-layouts  5.4 us

profile of v1, /device:TPU:27, one launch (start us, length us, event | category | flops | bytes accessed | tf_op | source)
XLA Modules:
  0.0 40.1 jit_solution(12543751070175354627)
XLA Ops:
  0.6 0.0 copy-start
  0.6 1.0 %copy-done = bf16[4,64,576]{2,1,0:T(8,128)(2,1)S(1)} copy-done((bf16[4,64,576]{2,1,0:T(8,128)(2,1)S(1)}, bf16[4,64,576]{2,1,0:T(8,128)(2,1)}, u32[]{:S(2)}) %copy-start) | copy-done | bytes 294936
  1.6 0.0 copy-start.1
  1.6 0.8 %copy-done.1 = f32[1,1,64,256]{3,2,1,0:T(8,128)S(1)} copy-done((f32[1,1,64,256]{3,2,1,0:T(8,128)S(1)}, f32[1,1,64,256]{3,2,1,0:T(8,128)}, u32[]{:S(2)}) %copy-start.1) | copy-done | bytes 65560
  2.4 0.0 copy-start.2
  2.4 0.8 %copy-done.2 = f32[1,1,64,256]{3,2,1,0:T(8,128)S(1)} copy-done((f32[1,1,64,256]{3,2,1,0:T(8,128)S(1)}, f32[1,1,64,256]{3,2,1,0:T(8,128)}, u32[]{:S(2)}) %copy-start.2) | copy-done | bytes 65560
  3.3 0.0 copy-start.3
  3.3 0.7 %copy-done.3 = f32[1,64]{1,0:T(1,128)S(1)} copy-done((f32[1,64]{1,0:T(1,128)S(1)}, f32[1,64]{1,0:T(1,128)}, u32[]{:S(2)}) %copy-start.3) | copy-done | bytes 280
  3.9 34.1 %shard_map.67 = (f32[1,1,64,256]{3,2,1,0:T(8,128)S(1)}, f32[1,1,64,256]{3,2,1,0:T(8,128)S(1)}, f32[4,64,576]{2,1,0:T(8,128)S(1)}) custom-call(f32[1,1,64,256]{3,2,1,0:T(8,128)S(1)} %copy-done.1, bf16[4,64,576]{2,1,0:T(8,128)(2,1)S(1)} %copy-done, f32[1,64]{1,0:T(1,128)S(1)} %copy-done.3, f32[1,1,64,256]{3,2,1,0:T(8,128)S(1)} %copy-done.2), custom_call_target="tpu_custom_call" | custom-call | tf_op jit(solution)/shard_map/pallas_call | solution.py:377
  38.0 0.6 %copy.10 = f32[1,1,64,256]{3,2,1,0:T(8,128)} copy(f32[1,1,64,256]{3,2,1,0:T(8,128)S(1)} %get-tuple-element.6) | data formatting | bytes 131072
  38.6 0.6 %copy.11 = f32[1,1,64,256]{3,2,1,0:T(8,128)} copy(f32[1,1,64,256]{3,2,1,0:T(8,128)S(1)} %get-tuple-element.7) | data formatting | bytes 131072
  39.3 0.8 %copy.12 = f32[4,64,576]{2,1,0:T(8,128)} copy(f32[4,64,576]{2,1,0:T(8,128)S(1)} %get-tuple-element.8) | data formatting | bytes 1179648
Async XLA Ops:
  0.6 1.0 %copy-start = (bf16[4,64,576]{2,1,0:T(8,128)(2,1)S(1)}, bf16[4,64,576]{2,1,0:T(8,128)(2,1)}, u32[]{:S(2)}) copy-start(bf16[4,64,576]{2,1,0:T(8,128)(2,1)} %w_ref.1) | copy-start | bytes 884740
  1.6 0.8 %copy-start.1 = (f32[1,1,64,256]{3,2,1,0:T(8,128)S(1)}, f32[1,1,64,256]{3,2,1,0:T(8,128)}, u32[]{:S(2)}) copy-start(f32[1,1,64,256]{3,2,1,0:T(8,128)} %cp_ref.1) | copy-start | bytes 196612
  2.4 0.8 %copy-start.2 = (f32[1,1,64,256]{3,2,1,0:T(8,128)S(1)}, f32[1,1,64,256]{3,2,1,0:T(8,128)}, u32[]{:S(2)}) copy-start(f32[1,1,64,256]{3,2,1,0:T(8,128)} %cot_ref.1) | copy-start | bytes 196612
  3.3 0.7 %copy-start.3 = (f32[1,64]{1,0:T(1,128)S(1)}, f32[1,64]{1,0:T(1,128)}, u32[]{:S(2)}) copy-start(f32[1,64]{1,0:T(1,128)} %gain_ref.1) | copy-start | bytes 772

commit v2 on v1

--- a/solution.py
+++ b/solution.py
@@ -15,13 +15,20 @@
 def kernel(
     depth,
     dp,
+    cp_hbm,
+    w_hbm,
+    gain_hbm,
+    cot_hbm,
+    corr_ref,
+    gcp_ref,
+    gw_ref,
     cp_ref,
     w_ref,
     gain_ref,
     cot_ref,
-    corr_ref,
-    gcp_ref,
-    gw_ref,
+    in_sem,
+    out_sem,
+    gcp_buf,
     patches,
     slopes,
     back_patches,
@@ -59,6 +66,17 @@
 ):
     layers, channels, width = w_ref.shape
     pixels = cp_ref.shape[-1]
+    fetches = [
+        pltpu.make_async_copy(cp_hbm, cp_ref, in_sem.at[0]),
+        pltpu.make_async_copy(gain_hbm, gain_ref, in_sem.at[1]),
+        pltpu.make_async_copy(cot_hbm, cot_ref, in_sem.at[2]),
+    ]
+    for layer in range(layers):
+        fetches.append(
+            pltpu.make_async_copy(w_hbm.at[layer], w_ref.at[layer], in_sem.at[3 + layer])
+        )
+    for fetch in fetches:
+        fetch.start()
     half = channels // 2
     step_size = 1.0 / (layers * depth)
     hops = []
@@ -87,19 +105,20 @@
         def _():
             pl.semaphore_signal(barrier, inc=1, device_id={"depth": me - hop}, device_id_type=MESH)
 
-    pixel = lax.broadcasted_iota(jnp.int32, (1, pixels), 1)
+    pixel = lax.broadcasted_iota(jnp.int32, (8, pixels), 1)
     row, column = pixel // WID, pixel % WID
     masks = []
     for a, b in TAP_OFFSETS:
         ok = (row + a >= 0) & (row + a < pixels // WID) & (column + b >= 0) & (column + b < WID)
-        masks.append(jnp.broadcast_to(ok, (channels, pixels)))
+        masks.append(jnp.where(ok, 1.0, 0.0)[None])
 
     def unfold(values, ref):
         for t, (a, b) in enumerate(TAP_OFFSETS):
             off = a * WID + b
             moved = values
             if off:
-                moved = jnp.where(masks[t], pltpu.roll(values, (-off) % pixels, 1), 0.0)
+                moved = pltpu.roll(values, (-off) % pixels, 1).reshape(channels // 8, 8, pixels)
+                moved = (moved * masks[t]).reshape(channels, pixels)
             ref[t * channels : (t + 1) * channels, :] = moved.astype(jnp.bfloat16)
 
     def forward_layer(u, layer, which):
@@ -206,15 +225,20 @@
             fwd[r + 1] = fwd[r]
 
     gains[0] = jnp.zeros_like(gains[0])
+    fetches[1].wait()
     gains[0, 0:1, 0:channels] = gain_ref[...]
     passed_buf[...] = jnp.zeros_like(passed_buf)
+    fetches[0].wait()
     own = cp_ref[0, 0]
+    fetches[3].wait()
     u = forward_layer(own, 0, 0)
     pl.semaphore_wait(barrier, count)
+    fetches[2].wait()
     start_adj(0)
     if rounds > 1:
         start_gain(0)
     for layer in range(1, layers):
+        fetches[3 + layer].wait()
         u = forward_layer(u, layer, 0)
     relaxed_buf[...] = u
 
@@ -273,7 +297,8 @@
         take_fwd(r)
         if r + 1 < rounds:
             start_fwd(r + 1)
-    corr_ref[0, 0] = fwd[rounds]
+    put_corr = pltpu.make_async_copy(fwd.at[rounds], corr_ref.at[0, 0], out_sem.at[0])
+    put_corr.start()
 
     @pl.when(me + 1 < depth)
     def _():
@@ -320,7 +345,12 @@
         b_copy(layer).wait_recv()
         sum_b[layer] = sum_a[layer] + part_b[layer]
         c_copy(layer).start()
-        gw_ref[layer, mine, :] = sum_b[layer]
+        put_own(layer).start()
+
+    def put_own(layer):
+        return pltpu.make_async_copy(
+            sum_b.at[layer], gw_ref.at[layer, mine], out_sem.at[2 + layer]
+        )
 
     for layer in reversed(range(layers)):
         g, grads = backward_layer(g, layer, 0)
@@ -328,16 +358,21 @@
         a_copy(layer).start()
         if layer + 1 < layers:
             middle(layer + 1)
-    gcp_ref[0, 0] = g + jnp.where(me == 0, 1.0, 0.0) * back_buf[...]
+    gcp_buf[...] = g + jnp.where(me == 0, 1.0, 0.0) * back_buf[...]
+    put_gcp = pltpu.make_async_copy(gcp_buf, gcp_ref.at[0, 0], out_sem.at[1])
+    put_gcp.start()
     middle(0)
     for layer in reversed(range(layers)):
         last(layer)
     for layer in reversed(range(layers)):
         c_copy(layer).wait_recv()
+        put_own(layer).wait()
         a_copy(layer).wait_send()
         b_copy(layer).wait_send()
         c_copy(layer).wait_send()
 
+    put_corr.wait()
+    put_gcp.wait()
     for r in range(rounds):
         if r + 1 < rounds:
 
@@ -360,6 +395,21 @@
     @pl.when(me > 0)
     def _():
         back_copy().wait_send()
+
+
+def deliver(corr_in, gcp_in, gw_in, corr_out, gcp_out, gw_out, sem):
+    moves = [
+        pltpu.make_async_copy(corr_in, corr_out, sem.at[0]),
+        pltpu.make_async_copy(gcp_in, gcp_out, sem.at[1]),
+    ]
+    for layer in range(gw_in.shape[0]):
+        moves.append(
+            pltpu.make_async_copy(gw_in.at[layer], gw_out.at[layer], sem.at[2 + layer])
+        )
+    for move in moves:
+        move.start()
+    for move in moves:
+        move.wait()
 
 
 def solution(mesh):
@@ -373,17 +423,25 @@
         half = (layers, channels // 2, width)
         f32, bf16 = jnp.float32, jnp.bfloat16
         dma = pltpu.SemaphoreType.DMA
-        vmem = pl.BlockSpec(memory_space=pltpu.VMEM)
-        return pl.pallas_call(
+        hbm = pl.BlockSpec(memory_space=pltpu.HBM)
+        results = (
+            jax.ShapeDtypeStruct(cpoints.shape, f32),
+            jax.ShapeDtypeStruct(cpoints.shape, f32),
+            jax.ShapeDtypeStruct(weights.shape, f32),
+        )
+        found = pl.pallas_call(
             functools.partial(kernel, depth, dp),
-            out_shape=(
-                jax.ShapeDtypeStruct(cpoints.shape, f32),
-                jax.ShapeDtypeStruct(cpoints.shape, f32),
-                jax.ShapeDtypeStruct(weights.shape, f32),
-            ),
-            in_specs=[vmem] * 4,
-            out_specs=(vmem,) * 3,
+            out_shape=results,
+            in_specs=[hbm] * 4,
+            out_specs=(hbm,) * 3,
             scratch_shapes=[
+                pltpu.VMEM(cpoints.shape, f32),
+                pltpu.VMEM(weights.shape, bf16),
+                pltpu.VMEM(coarse_gain.shape, f32),
+                pltpu.VMEM(cotangent.shape, f32),
+                dma((3 + layers,)),
+                dma((2 + layers,)),
+                pltpu.VMEM(state, f32),
                 pltpu.VMEM((2, layers, width, pixels), bf16),
                 pltpu.VMEM((2, layers) + state, f32),
                 pltpu.VMEM((width, pixels), bf16),
@@ -420,9 +478,17 @@
                 dma((layers,)),
             ],
             compiler_params=pltpu.CompilerParams(
-                collective_id=0, has_side_effects=True, vmem_limit_bytes=40 * 1024 * 1024
+                collective_id=0, has_side_effects=True, vmem_limit_bytes=60 * 1024 * 1024
             ),
         )(cpoints, weights, coarse_gain, cotangent)
+        return pl.pallas_call(
+            deliver,
+            out_shape=results,
+            in_specs=[hbm] * 3,
+            out_specs=(hbm,) * 3,
+            scratch_shapes=[dma((2 + layers,))],
+            compiler_params=pltpu.CompilerParams(vmem_limit_bytes=60 * 1024 * 1024),
+        )(*found)
 
     states = P("depth", "dp", None, None)
     blocks = P("depth", None, None)

time: 40.4 us -> 61 us (1.51)
  Pallas kernels: 34.1 us -> 60.2 us
  local copies, waits for them, and re-layouts: 5.4 us -> 0 us
    pallas_call x1 -> x2, Pallas kernels: 34.1 us -> 60.2 us  [the longest x1 35.2 us: step(): pl.pallas_call(functools.partial(kernel, depth, dp), out_shape=results, i...]
    unnamed x11 -> x0, local copies, waits for them, and re-layouts: 5.4 us -> none
where the time goes in v2:
time: 61 us; the launch traced here: 60.8 us
  Pallas kernels  60.2 us (99%)
  between operations  0.64 us (1%)
    pallas_call x1, Pallas kernels, step(): pl.pallas_call(functools.partial(kernel, depth, dp), out_shape=results, i...  35.2 us
    pallas_call x1, Pallas kernels, step(): pl.pallas_call(deliver, out_shape=results, in_specs=[hbm] * 3, out_specs=...  25 us

profile of v2, /device:TPU:27, one launch (start us, length us, event | category | flops | bytes accessed | tf_op | source)
XLA Modules:
  0.0 60.8 jit_solution(7610706251041783638)
XLA Ops:
  0.6 35.2 %shard_map.67 = (f32[1,1,64,256]{3,2,1,0:T(8,128)}, f32[1,1,64,256]{3,2,1,0:T(8,128)}, f32[4,64,576]{2,1,0:T(8,128)}) custom-call(f32[1,1,64,256]{3,2,1,0:T(8,128)} %cp_hbm.1, bf16[4,64,576]{2,1,0:T(8,128)(2,1)} %w_hbm.1, f32[1,64]{1,0:T(1,128)} %gain_hbm.1, f32[1,1,64,256]{3,2,1,0:T(8,128)} %cot_hbm.1), custom_call_target="tpu_custom_call" | custom-call | tf_op jit(solution)/shard_map/pallas_call | solution.py:432
  35.8 25.0 %shard_map.68 = (f32[1,1,64,256]{3,2,1,0:T(8,128)}, f32[1,1,64,256]{3,2,1,0:T(8,128)}, f32[4,64,576]{2,1,0:T(8,128)}) custom-call(f32[1,1,64,256]{3,2,1,0:T(8,128)} %get-tuple-element.6.corr_in, f32[1,1,64,256]{3,2,1,0:T(8,128)} %get-tuple-element.7.gcp_in, f32[4,64,576]{2,1,0:T(8,128)} %get-tuple-element.8.gw_in), custom_call_target="tpu_custom_call" | custom-call | tf_op jit(solution)/shard_map/pallas_call | solution.py:484

commit v3 on v2

--- a/solution.py
+++ b/solution.py
@@ -27,8 +27,6 @@
     gain_ref,
     cot_ref,
     in_sem,
-    out_sem,
-    gcp_buf,
     patches,
     slopes,
     back_patches,
@@ -297,8 +295,7 @@
         take_fwd(r)
         if r + 1 < rounds:
             start_fwd(r + 1)
-    put_corr = pltpu.make_async_copy(fwd.at[rounds], corr_ref.at[0, 0], out_sem.at[0])
-    put_corr.start()
+    corr_ref[0, 0] = fwd[rounds]
 
     @pl.when(me + 1 < depth)
     def _():
@@ -345,12 +342,7 @@
         b_copy(layer).wait_recv()
         sum_b[layer] = sum_a[layer] + part_b[layer]
         c_copy(layer).start()
-        put_own(layer).start()
-
-    def put_own(layer):
-        return pltpu.make_async_copy(
-            sum_b.at[layer], gw_ref.at[layer, mine], out_sem.at[2 + layer]
-        )
+        gw_ref[layer, mine, :] = sum_b[layer]
 
     for layer in reversed(range(layers)):
         g, grads = backward_layer(g, layer, 0)
@@ -358,21 +350,16 @@
         a_copy(layer).start()
         if layer + 1 < layers:
             middle(layer + 1)
-    gcp_buf[...] = g + jnp.where(me == 0, 1.0, 0.0) * back_buf[...]
-    put_gcp = pltpu.make_async_copy(gcp_buf, gcp_ref.at[0, 0], out_sem.at[1])
-    put_gcp.start()
+    gcp_ref[0, 0] = g + jnp.where(me == 0, 1.0, 0.0) * back_buf[...]
     middle(0)
     for layer in reversed(range(layers)):
         last(layer)
     for layer in reversed(range(layers)):
         c_copy(layer).wait_recv()
-        put_own(layer).wait()
         a_copy(layer).wait_send()
         b_copy(layer).wait_send()
         c_copy(layer).wait_send()
 
-    put_corr.wait()
-    put_gcp.wait()
     for r in range(rounds):
         if r + 1 < rounds:
 
@@ -423,6 +410,7 @@
         half = (layers, channels // 2, width)
         f32, bf16 = jnp.float32, jnp.bfloat16
         dma = pltpu.SemaphoreType.DMA
+        vmem = pl.BlockSpec(memory_space=pltpu.VMEM)
         hbm = pl.BlockSpec(memory_space=pltpu.HBM)
         results = (
             jax.ShapeDtypeStruct(cpoints.shape, f32),
@@ -433,15 +421,13 @@
             functools.partial(kernel, depth, dp),
             out_shape=results,
             in_specs=[hbm] * 4,
-            out_specs=(hbm,) * 3,
+            out_specs=(vmem,) * 3,
             scratch_shapes=[
                 pltpu.VMEM(cpoints.shape, f32),
                 pltpu.VMEM(weights.shape, bf16),
                 pltpu.VMEM(coarse_gain.shape, f32),
                 pltpu.VMEM(cotangent.shape, f32),
                 dma((3 + layers,)),
-                dma((2 + layers,)),
-                pltpu.VMEM(state, f32),
                 pltpu.VMEM((2, layers, width, pixels), bf16),
                 pltpu.VMEM((2, layers) + state, f32),
                 pltpu.VMEM((width, pixels), bf16),
@@ -478,16 +464,19 @@
                 dma((layers,)),
             ],
             compiler_params=pltpu.CompilerParams(
-                collective_id=0, has_side_effects=True, vmem_limit_bytes=60 * 1024 * 1024
+                collective_id=0, has_side_effects=True, vmem_limit_bytes=40 * 1024 * 1024
             ),
-        )(cpoints, weights, coarse_gain, cotangent)
+        )(*[
+            pltpu.with_memory_space_constraint(x, pltpu.HBM)
+            for x in (cpoints, weights, coarse_gain, cotangent)
+        ])
         return pl.pallas_call(
             deliver,
             out_shape=results,
-            in_specs=[hbm] * 3,
+            in_specs=[vmem] * 3,
             out_specs=(hbm,) * 3,
             scratch_shapes=[dma((2 + layers,))],
-            compiler_params=pltpu.CompilerParams(vmem_limit_bytes=60 * 1024 * 1024),
+            compiler_params=pltpu.CompilerParams(vmem_limit_bytes=8 * 1024 * 1024),
         )(*found)
 
     states = P("depth", "dp", None, None)

time: 61 us -> 36.7 us (0.60)
  Pallas kernels: 60.2 us -> 35.9 us
    pallas_call x1, Pallas kernels: 25 us -> 0.93 us  [step(): pl.pallas_call(deliver, out_shape=results, in_specs=[vmem] * 3, out_specs...]
where the time goes in v3:
time: 36.7 us; the launch traced here: 36.6 us
  Pallas kernels  35.9 us (98%)
  between operations  0.64 us (2%)
    pallas_call x1, Pallas kernels, step(): pl.pallas_call(functools.partial(kernel, depth, dp), out_shape=results, i...  35 us
    pallas_call x1, Pallas kernels, step(): pl.pallas_call(deliver, out_shape=results, in_specs=[vmem] * 3, out_specs...  0.93 us

profile of v3, /device:TPU:27, one launch (start us, length us, event | category | flops | bytes accessed | tf_op | source)
XLA Modules:
  0.0 36.6 jit_solution(333367812595070412)
XLA Ops:
  0.6 35.0 %shard_map.67 = (f32[1,1,64,256]{3,2,1,0:T(8,128)S(1)}, f32[1,1,64,256]{3,2,1,0:T(8,128)S(1)}, f32[4,64,576]{2,1,0:T(8,128)S(1)}) custom-call(f32[1,1,64,256]{3,2,1,0:T(8,128)} %cp_hbm.1, bf16[4,64,576]{2,1,0:T(8,128)(2,1)} %w_hbm.1, f32[1,64]{1,0:T(1,128)} %gain_hbm.1, f32[1,1,64,256]{3,2,1,0:T(8,128)} %cot_hbm.1), custom_call_target="tpu_custom_call" | custom-call | tf_op jit(solution)/shard_map/pallas_call | solution.py:420
  35.6 0.9 %shard_map.68 = (f32[1,1,64,256]{3,2,1,0:T(8,128)}, f32[1,1,64,256]{3,2,1,0:T(8,128)}, f32[4,64,576]{2,1,0:T(8,128)}) custom-call(f32[1,1,64,256]{3,2,1,0:T(8,128)S(1)} %get-tuple-element.6.corr_in, f32[1,1,64,256]{3,2,1,0:T(8,128)S(1)} %get-tuple-element.7.gcp_in, f32[4,64,576]{2,1,0:T(8,128)S(1)} %get-tuple-element.8.gw_in), custom_call_target="tpu_custom_call" | custom-call | tf_op jit(solution)/shard_map/pallas_call | solution.py:473

commit v4 on v3

--- a/solution.py
+++ b/solution.py
@@ -244,15 +244,8 @@
     def _():
         relaxed_copy().start()
 
-    for r in range(rounds - 1):
-        take_gain(r)
-        if r + 1 < rounds - 1:
-            start_gain(r + 1)
-        take_adj(r)
-        start_adj(r + 1)
-
     one = jnp.where(eye, 1.0, 0.0).astype(jnp.bfloat16)
-    for layer in range(layers):
+    def turn(layer):
         pieces = []
         for t in reversed(range(len(TAP_OFFSETS))):
             block = w_ref[layer, :, t * channels : (t + 1) * channels]
@@ -263,6 +256,17 @@
             )
         turned[layer] = jnp.concatenate(pieces, axis=1)
 
+    turn(0)
+    for r in range(rounds - 1):
+        take_gain(r)
+        if r + 1 < rounds - 1:
+            start_gain(r + 1)
+        take_adj(r)
+        start_adj(r + 1)
+        if r == 0:
+            for layer in range(1, layers):
+                turn(layer)
+
     @pl.when(me > 0)
     def _():
         relaxed_back = along(
@@ -285,17 +289,19 @@
     for position, layer in enumerate(reversed(range(layers))):
         g, grads = backward_layer(g, layer, 1)
         start_grads[layer] = grads
+        if position == layers - 2:
+            take_fwd(0)
+            if rounds > 1:
+                start_fwd(1)
     back_buf[...] = g
 
     @pl.when(me > 0)
     def _():
         back_copy().start()
 
-    for r in range(rounds):
+    for r in range(1, rounds - 1):
         take_fwd(r)
-        if r + 1 < rounds:
-            start_fwd(r + 1)
-    corr_ref[0, 0] = fwd[rounds]
+        start_fwd(r + 1)
 
     @pl.when(me + 1 < depth)
     def _():
@@ -351,6 +357,9 @@
         if layer + 1 < layers:
             middle(layer + 1)
     gcp_ref[0, 0] = g + jnp.where(me == 0, 1.0, 0.0) * back_buf[...]
+    if rounds > 1:
+        take_fwd(rounds - 1)
+    corr_ref[0, 0] = fwd[rounds]
     middle(0)
     for layer in reversed(range(layers)):
         last(layer)

time: 36.7 us -> 35.9 us (0.978)
  the two profiles are of different devices: /device:TPU:27 before, /device:TPU:0 now
where the time goes in v4:
time: 35.9 us; the launch traced here: 35.7 us
  Pallas kernels  35.1 us (98%)
  between operations  0.64 us (2%)
    pallas_call x1, Pallas kernels, step(): pl.pallas_call(functools.partial(kernel, depth, dp), out_shape=results, i...  34.1 us
    pallas_call x1, Pallas kernels, step(): pl.pallas_call(deliver, out_shape=results, in_specs=[vmem] * 3, out_specs...  0.93 us

profile of v4, /device:TPU:0, one launch (start us, length us, event | category | flops | bytes accessed | tf_op | source)
XLA Modules:
  0.0 35.7 jit_solution(233149311025857215)
XLA Ops:
  0.6 34.1 %shard_map.67 = (f32[1,1,64,256]{3,2,1,0:T(8,128)S(1)}, f32[1,1,64,256]{3,2,1,0:T(8,128)S(1)}, f32[4,64,576]{2,1,0:T(8,128)S(1)}) custom-call(f32[1,1,64,256]{3,2,1,0:T(8,128)} %cp_hbm.1, bf16[4,64,576]{2,1,0:T(8,128)(2,1)} %w_hbm.1, f32[1,64]{1,0:T(1,128)} %gain_hbm.1, f32[1,1,64,256]{3,2,1,0:T(8,128)} %cot_hbm.1), custom_call_target="tpu_custom_call" | custom-call | tf_op jit(solution)/shard_map/pallas_call | solution.py:429
  34.8 0.9 %shard_map.68 = (f32[1,1,64,256]{3,2,1,0:T(8,128)}, f32[1,1,64,256]{3,2,1,0:T(8,128)}, f32[4,64,576]{2,1,0:T(8,128)}) custom-call(f32[1,1,64,256]{3,2,1,0:T(8,128)S(1)} %get-tuple-element.6.corr_in, f32[1,1,64,256]{3,2,1,0:T(8,128)S(1)} %get-tuple-element.7.gcp_in, f32[4,64,576]{2,1,0:T(8,128)S(1)} %get-tuple-element.8.gw_in), custom_call_target="tpu_custom_call" | custom-call | tf_op jit(solution)/shard_map/pallas_call | solution.py:482

commit v5 on v4

--- a/solution.py
+++ b/solution.py
@@ -9,7 +9,6 @@
 
 MESH = pl.DeviceIdType.MESH
 WID = 16
-TAP_OFFSETS = [(-1, -1), (-1, 0), (-1, 1), (0, -1), (0, 0), (0, 1), (1, -1), (1, 0), (1, 1)]
 
 
 def kernel(
@@ -30,6 +29,8 @@
     patches,
     slopes,
     back_patches,
+    back_rows,
+    stacked,
     turned,
     start_grads,
     relaxed_buf,
@@ -105,41 +106,57 @@
 
     pixel = lax.broadcasted_iota(jnp.int32, (8, pixels), 1)
     row, column = pixel // WID, pixel % WID
-    masks = []
-    for a, b in TAP_OFFSETS:
-        ok = (row + a >= 0) & (row + a < pixels // WID) & (column + b >= 0) & (column + b < WID)
-        masks.append(jnp.where(ok, 1.0, 0.0)[None])
-
-    def unfold(values, ref):
-        for t, (a, b) in enumerate(TAP_OFFSETS):
-            off = a * WID + b
-            moved = values
-            if off:
-                moved = pltpu.roll(values, (-off) % pixels, 1).reshape(channels // 8, 8, pixels)
-                moved = (moved * masks[t]).reshape(channels, pixels)
-            ref[t * channels : (t + 1) * channels, :] = moved.astype(jnp.bfloat16)
+    row_ok, column_ok = {}, {}
+    for a in (-1, 1):
+        row_ok[a] = jnp.where((row + a >= 0) & (row + a < pixels // WID), 1.0, 0.0)[None]
+        column_ok[a] = jnp.where((column + a >= 0) & (column + a < WID), 1.0, 0.0)[None]
+    tall = 3 * channels
+    blocks = [slice(n * channels, (n + 1) * channels) for n in range(3)]
+
+    def moved(values, distance, mask):
+        shifted = pltpu.roll(values, (-distance) % pixels, 1).reshape(channels // 8, 8, pixels)
+        return (shifted * mask).reshape(channels, pixels)
+
+    def by_rows(values, a):
+        return moved(values, a * WID, row_ok[a])
+
+    def by_columns(values, b):
+        return moved(values, b, column_ok[b])
 
     def forward_layer(u, layer, which):
         squashed = jnp.tanh(u)
         slopes[which, layer] = 1.0 - squashed * squashed
-        unfold(squashed, patches.at[which, layer])
-        mixed = jnp.dot(
-            w_ref[layer], patches[which, layer], preferred_element_type=jnp.float32
-        )
+        kept = patches.at[which, layer]
+        kept[blocks[0], :] = by_columns(squashed, -1).astype(jnp.bfloat16)
+        kept[blocks[1], :] = squashed.astype(jnp.bfloat16)
+        kept[blocks[2], :] = by_columns(squashed, 1).astype(jnp.bfloat16)
+        mixed = jnp.dot(stacked[layer], kept[...], preferred_element_type=jnp.float32)
+        mixed = mixed[blocks[1]] + by_rows(mixed[blocks[0]], -1) + by_rows(mixed[blocks[2]], 1)
         return u + step_size * mixed
 
     def backward_layer(g, layer, which):
-        scaled = step_size * g
-        rounded = scaled.astype(jnp.bfloat16)
-        unfold(rounded.astype(jnp.float32), back_patches)
+        rounded = (step_size * g).astype(jnp.bfloat16)
+        wide = rounded.astype(jnp.float32)
+        back_patches[blocks[0], :] = by_columns(wide, 1).astype(jnp.bfloat16)
+        back_patches[blocks[1], :] = rounded
+        back_patches[blocks[2], :] = by_columns(wide, -1).astype(jnp.bfloat16)
+        spread = jnp.dot(turned[layer], back_patches[...], preferred_element_type=jnp.float32)
+        back_rows[blocks[0], :] = by_rows(wide, 1).astype(jnp.bfloat16)
+        back_rows[blocks[1], :] = rounded
+        back_rows[blocks[2], :] = by_rows(wide, -1).astype(jnp.bfloat16)
         grads = lax.dot_general(
-            rounded,
+            back_rows[...],
             patches[which, layer],
             (((1,), (1,)), ((), ())),
             preferred_element_type=jnp.float32,
         )
-        spread = jnp.dot(turned[layer], back_patches[...], preferred_element_type=jnp.float32)
+        grads = jnp.concatenate([grads[block] for block in blocks], axis=1)
+        spread = spread[blocks[1]] + by_rows(spread[blocks[0]], 1) + by_rows(spread[blocks[2]], -1)
         return g + slopes[which, layer] * spread, grads
+
+    def stack(layer):
+        for n in range(3):
+            stacked[layer, blocks[n], :] = w_ref[layer, :, n * tall : (n + 1) * tall]
 
     def along(src, dst, send, recv, target):
         return pltpu.make_async_remote_copy(
@@ -229,6 +246,7 @@
     fetches[0].wait()
     own = cp_ref[0, 0]
     fetches[3].wait()
+    stack(0)
     u = forward_layer(own, 0, 0)
     pl.semaphore_wait(barrier, count)
     fetches[2].wait()
@@ -237,6 +255,7 @@
         start_gain(0)
     for layer in range(1, layers):
         fetches[3 + layer].wait()
+        stack(layer)
         u = forward_layer(u, layer, 0)
     relaxed_buf[...] = u
 
@@ -244,17 +263,22 @@
     def _():
         relaxed_copy().start()
 
-    one = jnp.where(eye, 1.0, 0.0).astype(jnp.bfloat16)
+    one = lax.broadcasted_iota(jnp.int32, (tall, tall), 0) == lax.broadcasted_iota(
+        jnp.int32, (tall, tall), 1
+    )
+    one = jnp.where(one, 1.0, 0.0).astype(jnp.bfloat16)
+
     def turn(layer):
-        pieces = []
-        for t in reversed(range(len(TAP_OFFSETS))):
-            block = w_ref[layer, :, t * channels : (t + 1) * channels]
-            pieces.append(
-                lax.dot_general(
-                    one, block, (((1,), (1,)), ((), ())), preferred_element_type=jnp.float32
-                ).astype(jnp.bfloat16)
+        for n in range(3):
+            flipped = lax.dot_general(
+                one,
+                stacked[layer, blocks[n], :],
+                (((1,), (1,)), ((), ())),
+                preferred_element_type=jnp.float32,
             )
-        turned[layer] = jnp.concatenate(pieces, axis=1)
+            turned[layer, blocks[n], :] = jnp.concatenate(
+                [flipped[block] for block in blocks], axis=1
+            ).astype(jnp.bfloat16)
 
     turn(0)
     for r in range(rounds - 1):
@@ -437,10 +461,12 @@
                 pltpu.VMEM(coarse_gain.shape, f32),
                 pltpu.VMEM(cotangent.shape, f32),
                 dma((3 + layers,)),
-                pltpu.VMEM((2, layers, width, pixels), bf16),
+                pltpu.VMEM((2, layers, width // 3, pixels), bf16),
                 pltpu.VMEM((2, layers) + state, f32),
-                pltpu.VMEM((width, pixels), bf16),
-                pltpu.VMEM((layers, channels, width), bf16),
+                pltpu.VMEM((width // 3, pixels), bf16),
+                pltpu.VMEM((width // 3, pixels), bf16),
+                pltpu.VMEM((layers, 3 * channels, width // 3), bf16),
+                pltpu.VMEM((layers, 3 * channels, width // 3), bf16),
                 pltpu.VMEM((layers, channels, width), f32),
                 pltpu.VMEM(state, f32),
                 pltpu.VMEM(state, f32),

time: 35.9 us -> 35.9 us (level)
  no operation moved by 1% of the time
where the time goes in v5:
time: 35.9 us; the launch traced here: 35.8 us
  Pallas kernels  35.1 us (98%)
  between operations  0.64 us (2%)
    pallas_call x1, Pallas kernels, step(): pl.pallas_call(functools.partial(kernel, depth, dp), out_shape=results, i...  34.2 us
    pallas_call x1, Pallas kernels, step(): pl.pallas_call(deliver, out_shape=results, in_specs=[vmem] * 3, out_specs...  0.93 us

profile of v5, /device:TPU:0, one launch (start us, length us, event | category | flops | bytes accessed | tf_op | source)
XLA Modules:
  0.0 35.8 jit_solution(12289255649817719125)
XLA Ops:
  0.6 34.2 %shard_map.67 = (f32[1,1,64,256]{3,2,1,0:T(8,128)S(1)}, f32[1,1,64,256]{3,2,1,0:T(8,128)S(1)}, f32[4,64,576]{2,1,0:T(8,128)S(1)}) custom-call(f32[1,1,64,256]{3,2,1,0:T(8,128)} %cp_hbm.1, bf16[4,64,576]{2,1,0:T(8,128)(2,1)} %w_hbm.1, f32[1,64]{1,0:T(1,128)} %gain_hbm.1, f32[1,1,64,256]{3,2,1,0:T(8,128)} %cot_hbm.1), custom_call_target="tpu_custom_call" | custom-call | tf_op jit(solution)/shard_map/pallas_call | solution.py:453
  34.9 0.9 %shard_map.68 = (f32[1,1,64,256]{3,2,1,0:T(8,128)}, f32[1,1,64,256]{3,2,1,0:T(8,128)}, f32[4,64,576]{2,1,0:T(8,128)}) custom-call(f32[1,1,64,256]{3,2,1,0:T(8,128)S(1)} %get-tuple-element.6.corr_in, f32[1,1,64,256]{3,2,1,0:T(8,128)S(1)} %get-tuple-element.7.gcp_in, f32[4,64,576]{2,1,0:T(8,128)S(1)} %get-tuple-element.8.gw_in), custom_call_target="tpu_custom_call" | custom-call | tf_op jit(solution)/shard_map/pallas_call | solution.py:508

commit v6 on v5

--- a/solution.py
+++ b/solution.py
@@ -28,11 +28,20 @@
     in_sem,
     patches,
     slopes,
-    back_patches,
-    back_rows,
+    both_patches,
+    both_rows,
     stacked,
     turned,
     start_grads,
+    own_grads,
+    mate_cp,
+    mate_passed,
+    mate_bar,
+    part_d,
+    mate_send,
+    mate_recv,
+    d_send,
+    d_recv,
     relaxed_buf,
     start_buf,
     back_buf,
@@ -104,6 +113,20 @@
         def _():
             pl.semaphore_signal(barrier, inc=1, device_id={"depth": me - hop}, device_id_type=MESH)
 
+    count = count + jnp.where(me + 1 < depth, 1, 0) + jnp.where(me > 0, 1, 0)
+
+    @pl.when(me + 1 < depth)
+    def _():
+        pl.semaphore_signal(
+            barrier, inc=1, device_id={"depth": me + 1, "dp": across}, device_id_type=MESH
+        )
+
+    @pl.when(me > 0)
+    def _():
+        pl.semaphore_signal(
+            barrier, inc=1, device_id={"depth": me - 1, "dp": across}, device_id_type=MESH
+        )
+
     pixel = lax.broadcasted_iota(jnp.int32, (8, pixels), 1)
     row, column = pixel // WID, pixel % WID
     row_ok, column_ok = {}, {}
@@ -135,6 +158,7 @@
         return u + step_size * mixed
 
     def backward_layer(g, layer, which):
+        back_patches, back_rows = both_patches.at[which // 2], both_rows.at[which // 2]
         rounded = (step_size * g).astype(jnp.bfloat16)
         wide = rounded.astype(jnp.float32)
         back_patches[blocks[0], :] = by_columns(wide, 1).astype(jnp.bfloat16)
@@ -189,6 +213,19 @@
     def back_copy():
         return along(back_buf, bar_buf, edge_send.at[1], edge_recv.at[1], {"depth": me - 1})
 
+    def mate_cp_copy():
+        return along(
+            cp_ref.at[0, 0], mate_cp, mate_send.at[0], mate_recv.at[0], {"dp": across}
+        )
+
+    def mate_passed_copy():
+        return along(passed_buf, mate_passed, mate_send.at[1], mate_recv.at[1], {"dp": across})
+
+    def mate_back_copy():
+        return along(
+            back_buf, mate_bar, mate_send.at[2], mate_recv.at[2], {"depth": me - 1, "dp": across}
+        )
+
     eye = lax.broadcasted_iota(jnp.int32, (channels, channels), 0) == lax.broadcasted_iota(
         jnp.int32, (channels, channels), 1
     )
@@ -253,6 +290,7 @@
     start_adj(0)
     if rounds > 1:
         start_gain(0)
+    mate_cp_copy().start()
     for layer in range(1, layers):
         fetches[3 + layer].wait()
         stack(layer)
@@ -290,6 +328,10 @@
         if r == 0:
             for layer in range(1, layers):
                 turn(layer)
+            mate_cp_copy().wait_recv()
+            v = mate_cp[...]
+            for layer in range(layers):
+                v = forward_layer(v, layer, 2)
 
     @pl.when(me > 0)
     def _():
@@ -308,11 +350,63 @@
     fwd[0] = u - jnp.where(me == 0, 0.0, 1.0) * gain_column(0) * start_buf[...]
     start_fwd(0)
     take_adj(rounds - 1)
+    mate_passed_copy().start()
+
+    mine = pl.ds(pl.multiple_of(side * half, half), half)
+    other = pl.ds(pl.multiple_of((1 - side) * half, half), half)
+
+    def a_copy(layer):
+        return along(
+            start_grads.at[layer, other],
+            part_a.at[layer],
+            a_send.at[layer],
+            a_recv.at[layer],
+            {"dp": sibling},
+        )
+
+    def b_copy(layer):
+        return along(
+            sum_a.at[layer], part_b.at[layer], b_send.at[layer], b_recv.at[layer], {"dp": across}
+        )
+
+    def c_copy(layer):
+        return along(
+            sum_b.at[layer],
+            gw_ref.at[layer, mine],
+            c_send.at[layer],
+            c_recv.at[layer],
+            {"dp": sibling},
+        )
+
+    def middle(layer):
+        a_copy(layer).wait_recv()
+        sum_a[layer] = start_grads[layer, mine, :] + part_a[layer]
+        b_copy(layer).start()
+
+    def d_copy(layer):
+        return along(
+            own_grads.at[layer, other],
+            part_d.at[layer],
+            d_send.at[layer],
+            d_recv.at[layer],
+            {"dp": sibling},
+        )
+
+    def last(layer):
+        b_copy(layer).wait_recv()
+        starts = sum_a[layer] + part_b[layer]
+        d_copy(layer).wait_recv()
+        sum_b[layer] = starts + (own_grads[layer, mine, :] + part_d[layer])
+        c_copy(layer).start()
+        gw_ref[layer, mine, :] = sum_b[layer]
 
     g = cot_ref[0, 0] + passed_buf[...]
     for position, layer in enumerate(reversed(range(layers))):
         g, grads = backward_layer(g, layer, 1)
         start_grads[layer] = grads
+        a_copy(layer).start()
+        if position == 2:
+            middle(layer + 2)
         if position == layers - 2:
             take_fwd(0)
             if rounds > 1:
@@ -322,7 +416,10 @@
     @pl.when(me > 0)
     def _():
         back_copy().start()
-
+        mate_back_copy().start()
+
+    for layer in reversed(range(layers - 1)):
+        middle(layer)
     for r in range(1, rounds - 1):
         take_fwd(r)
         start_fwd(r + 1)
@@ -330,61 +427,26 @@
     @pl.when(me + 1 < depth)
     def _():
         back_copy().wait_recv()
+        mate_back_copy().wait_recv()
 
     @pl.when(me + 1 == depth)
     def _():
         bar_buf[...] = jnp.zeros_like(bar_buf)
-
+        mate_bar[...] = jnp.zeros_like(mate_bar)
+
+    mate_passed_copy().wait_recv()
     g = bar_buf[...] - passed_buf[...]
-
-    mine = pl.ds(pl.multiple_of(side * half, half), half)
-    other = pl.ds(pl.multiple_of((1 - side) * half, half), half)
-
-    def a_copy(layer):
-        return along(
-            start_grads.at[layer, other],
-            part_a.at[layer],
-            a_send.at[layer],
-            a_recv.at[layer],
-            {"dp": sibling},
-        )
-
-    def b_copy(layer):
-        return along(
-            sum_a.at[layer], part_b.at[layer], b_send.at[layer], b_recv.at[layer], {"dp": across}
-        )
-
-    def c_copy(layer):
-        return along(
-            sum_b.at[layer],
-            gw_ref.at[layer, mine],
-            c_send.at[layer],
-            c_recv.at[layer],
-            {"dp": sibling},
-        )
-
-    def middle(layer):
-        a_copy(layer).wait_recv()
-        sum_a[layer] = start_grads[layer, mine, :] + part_a[layer]
-        b_copy(layer).start()
-
-    def last(layer):
-        b_copy(layer).wait_recv()
-        sum_b[layer] = sum_a[layer] + part_b[layer]
-        c_copy(layer).start()
-        gw_ref[layer, mine, :] = sum_b[layer]
+    h = mate_bar[...] - mate_passed[...]
 
     for layer in reversed(range(layers)):
         g, grads = backward_layer(g, layer, 0)
-        start_grads[layer] = start_grads[layer] + grads
-        a_copy(layer).start()
-        if layer + 1 < layers:
-            middle(layer + 1)
+        h, mate_grads = backward_layer(h, layer, 2)
+        own_grads[layer] = grads + mate_grads
+        d_copy(layer).start()
     gcp_ref[0, 0] = g + jnp.where(me == 0, 1.0, 0.0) * back_buf[...]
     if rounds > 1:
         take_fwd(rounds - 1)
     corr_ref[0, 0] = fwd[rounds]
-    middle(0)
     for layer in reversed(range(layers)):
         last(layer)
     for layer in reversed(range(layers)):
@@ -392,6 +454,9 @@
         a_copy(layer).wait_send()
         b_copy(layer).wait_send()
         c_copy(layer).wait_send()
+        d_copy(layer).wait_send()
+    mate_cp_copy().wait_send()
+    mate_passed_copy().wait_send()
 
     for r in range(rounds):
         if r + 1 < rounds:
@@ -415,6 +480,7 @@
     @pl.when(me > 0)
     def _():
         back_copy().wait_send()
+        mate_back_copy().wait_send()
 
 
 def deliver(corr_in, gcp_in, gw_in, corr_out, gcp_out, gw_out, sem):
@@ -461,13 +527,22 @@
                 pltpu.VMEM(coarse_gain.shape, f32),
                 pltpu.VMEM(cotangent.shape, f32),
                 dma((3 + layers,)),
-                pltpu.VMEM((2, layers, width // 3, pixels), bf16),
-                pltpu.VMEM((2, layers) + state, f32),
-                pltpu.VMEM((width // 3, pixels), bf16),
-                pltpu.VMEM((width // 3, pixels), bf16),
+                pltpu.VMEM((3, layers, width // 3, pixels), bf16),
+                pltpu.VMEM((3, layers) + state, f32),
+                pltpu.VMEM((2, width // 3, pixels), bf16),
+                pltpu.VMEM((2, width // 3, pixels), bf16),
                 pltpu.VMEM((layers, 3 * channels, width // 3), bf16),
                 pltpu.VMEM((layers, 3 * channels, width // 3), bf16),
                 pltpu.VMEM((layers, channels, width), f32),
+                pltpu.VMEM((layers, channels, width), f32),
+                pltpu.VMEM(state, f32),
+                pltpu.VMEM(state, f32),
+                pltpu.VMEM(state, f32),
+                pltpu.VMEM(half, f32),
+                dma((3,)),
+                dma((3,)),
+                dma((layers,)),
+                dma((layers,)),
                 pltpu.VMEM(state, f32),
                 pltpu.VMEM(state, f32),
                 pltpu.VMEM(state, f32),

time: 35.9 us -> 32.5 us (0.905)
  Pallas kernels: 35.1 us -> 31.7 us
    pallas_call x1, Pallas kernels: 34.2 us -> 30.8 us  [step(): pl.pallas_call(functools.partial(kernel, depth, dp), out_shape=results, i...]
where the time goes in v6:
time: 32.5 us; the launch traced here: 32.4 us
  Pallas kernels  31.7 us (98%)
  between operations  0.64 us (2%)
    pallas_call x1, Pallas kernels, step(): pl.pallas_call(functools.partial(kernel, depth, dp), out_shape=results, i...  30.8 us
    pallas_call x1, Pallas kernels, step(): pl.pallas_call(deliver, out_shape=results, in_specs=[vmem] * 3, out_specs...  0.93 us

profile of v6, /device:TPU:0, one launch (start us, length us, event | category | flops | bytes accessed | tf_op | source)
XLA Modules:
  0.0 32.4 jit_solution(11060897689682516666)
XLA Ops:
  0.6 30.8 %shard_map.67 = (f32[1,1,64,256]{3,2,1,0:T(8,128)S(1)}, f32[1,1,64,256]{3,2,1,0:T(8,128)S(1)}, f32[4,64,576]{2,1,0:T(8,128)S(1)}) custom-call(f32[1,1,64,256]{3,2,1,0:T(8,128)} %cp_hbm.1, bf16[4,64,576]{2,1,0:T(8,128)(2,1)} %w_hbm.1, f32[1,64]{1,0:T(1,128)} %gain_hbm.1, f32[1,1,64,256]{3,2,1,0:T(8,128)} %cot_hbm.1), custom_call_target="tpu_custom_call" | custom-call | tf_op jit(solution)/shard_map/pallas_call | solution.py:519
  31.5 0.9 %shard_map.68 = (f32[1,1,64,256]{3,2,1,0:T(8,128)}, f32[1,1,64,256]{3,2,1,0:T(8,128)}, f32[4,64,576]{2,1,0:T(8,128)}) custom-call(f32[1,1,64,256]{3,2,1,0:T(8,128)S(1)} %get-tuple-element.6.corr_in, f32[1,1,64,256]{3,2,1,0:T(8,128)S(1)} %get-tuple-element.7.gcp_in, f32[4,64,576]{2,1,0:T(8,128)S(1)} %get-tuple-element.8.gw_in), custom_call_target="tpu_custom_call" | custom-call | tf_op jit(solution)/shard_map/pallas_call | solution.py:583

commit v7 on v6

--- a/solution.py
+++ b/solution.py
@@ -197,9 +197,15 @@
             gains.at[r], gains_in.at[r], gain_send.at[r], gain_recv.at[r], {"depth": me + hops[r]}
         )
 
-    def adj_copy(r):
-        return along(
-            adj_out.at[r], adj_in.at[r], adj_send.at[r], adj_recv.at[r], {"depth": me - hops[r]}
+    parts = [slice(0, half), slice(half, channels)]
+
+    def adj_copy(r, n):
+        return along(
+            adj_out.at[r, parts[n]],
+            adj_in.at[r, parts[n]],
+            adj_send.at[r, n],
+            adj_recv.at[r, n],
+            {"depth": me - hops[r]},
         )
 
     def fwd_copy(r):
@@ -234,11 +240,12 @@
         line = jnp.broadcast_to(gains[r, 0:1, 0:channels], (channels, channels))
         return jnp.sum(jnp.where(eye, line, 0.0), axis=1, keepdims=True)
 
-    def start_adj(r):
+    def start_adj(r, n):
         @pl.when(me >= hops[r])
         def _():
-            adj_out[r] = gain_column(r) * (cot_ref[0, 0] + passed_buf[...])
-            adj_copy(r).start()
+            here = parts[n]
+            adj_out[r, here] = gain_column(r)[here] * (cot_ref[0, 0, here] + passed_buf[here])
+            adj_copy(r, n).start()
 
     def take_gain(r):
         @pl.when(me >= hops[r])
@@ -255,11 +262,12 @@
         def _():
             gain_copy(r).start()
 
-    def take_adj(r):
+    def take_adj(r, n):
         @pl.when(me + hops[r] < depth)
         def _():
-            adj_copy(r).wait_recv()
-            passed_buf[...] = passed_buf[...] + adj_in[r]
+            adj_copy(r, n).wait_recv()
+            here = parts[n]
+            passed_buf[here] = passed_buf[here] + adj_in[r, here]
 
     def start_fwd(r):
         @pl.when(me + hops[r] < depth)
@@ -287,7 +295,8 @@
     u = forward_layer(own, 0, 0)
     pl.semaphore_wait(barrier, count)
     fetches[2].wait()
-    start_adj(0)
+    for n in range(2):
+        start_adj(0, n)
     if rounds > 1:
         start_gain(0)
     mate_cp_copy().start()
@@ -323,15 +332,12 @@
         take_gain(r)
         if r + 1 < rounds - 1:
             start_gain(r + 1)
-        take_adj(r)
-        start_adj(r + 1)
+        for n in range(2):
+            take_adj(r, n)
+            start_adj(r + 1, n)
         if r == 0:
             for layer in range(1, layers):
                 turn(layer)
-            mate_cp_copy().wait_recv()
-            v = mate_cp[...]
-            for layer in range(layers):
-                v = forward_layer(v, layer, 2)
 
     @pl.when(me > 0)
     def _():
@@ -344,12 +350,16 @@
     def _():
         start_buf[...] = own
 
+    mate_cp_copy().wait_recv()
     u = start_buf[...]
+    v = mate_cp[...]
     for layer in range(layers):
         u = forward_layer(u, layer, 1)
+        v = forward_layer(v, layer, 2)
     fwd[0] = u - jnp.where(me == 0, 0.0, 1.0) * gain_column(0) * start_buf[...]
     start_fwd(0)
-    take_adj(rounds - 1)
+    for n in range(2):
+        take_adj(rounds - 1, n)
     mate_passed_copy().start()
 
     mine = pl.ds(pl.multiple_of(side * half, half), half)
@@ -444,11 +454,11 @@
         own_grads[layer] = grads + mate_grads
         d_copy(layer).start()
     gcp_ref[0, 0] = g + jnp.where(me == 0, 1.0, 0.0) * back_buf[...]
+    for layer in reversed(range(layers)):
+        last(layer)
     if rounds > 1:
         take_fwd(rounds - 1)
     corr_ref[0, 0] = fwd[rounds]
-    for layer in reversed(range(layers)):
-        last(layer)
     for layer in reversed(range(layers)):
         c_copy(layer).wait_recv()
         a_copy(layer).wait_send()
@@ -467,7 +477,8 @@
 
         @pl.when(me >= hops[r])
         def _():
-            adj_copy(r).wait_send()
+            for n in range(2):
+                adj_copy(r, n).wait_send()
 
         @pl.when(me + hops[r] < depth)
         def _():
@@ -560,8 +571,8 @@
                 pltpu.VMEM(half, f32),
                 dma((rounds,)),
                 dma((rounds,)),
-                dma((rounds,)),
-                dma((rounds,)),
+                dma((rounds, 2)),
+                dma((rounds, 2)),
                 dma((rounds,)),
                 dma((rounds,)),
                 dma((2,)),

time: 32.5 us -> 32 us (0.985)
  Pallas kernels: 31.7 us -> 31.2 us
    pallas_call x1, Pallas kernels: 30.8 us -> 30.2 us  [step(): pl.pallas_call(functools.partial(kernel, depth, dp), out_shape=results, i...]
where the time goes in v7:
time: 32 us; the launch traced here: 31.8 us
  Pallas kernels  31.2 us (98%)
  between operations  0.64 us (2%)
    pallas_call x1, Pallas kernels, step(): pl.pallas_call(functools.partial(kernel, depth, dp), out_shape=results, i...  30.2 us
    pallas_call x1, Pallas kernels, step(): pl.pallas_call(deliver, out_shape=results, in_specs=[vmem] * 3, out_specs...  0.93 us

profile of v7, /device:TPU:0, one launch (start us, length us, event | category | flops | bytes accessed | tf_op | source)
XLA Modules:
  0.0 31.8 jit_solution(10120477334479968613)
XLA Ops:
  0.6 30.2 %shard_map.67 = (f32[1,1,64,256]{3,2,1,0:T(8,128)S(1)}, f32[1,1,64,256]{3,2,1,0:T(8,128)S(1)}, f32[4,64,576]{2,1,0:T(8,128)S(1)}) custom-call(f32[1,1,64,256]{3,2,1,0:T(8,128)} %cp_hbm.1, bf16[4,64,576]{2,1,0:T(8,128)(2,1)} %w_hbm.1, f32[1,64]{1,0:T(1,128)} %gain_hbm.1, f32[1,1,64,256]{3,2,1,0:T(8,128)} %cot_hbm.1), custom_call_target="tpu_custom_call" | custom-call | tf_op jit(solution)/shard_map/pallas_call | solution.py:530
  30.9 0.9 %shard_map.68 = (f32[1,1,64,256]{3,2,1,0:T(8,128)}, f32[1,1,64,256]{3,2,1,0:T(8,128)}, f32[4,64,576]{2,1,0:T(8,128)}) custom-call(f32[1,1,64,256]{3,2,1,0:T(8,128)S(1)} %get-tuple-element.6.corr_in, f32[1,1,64,256]{3,2,1,0:T(8,128)S(1)} %get-tuple-element.7.gcp_in, f32[4,64,576]{2,1,0:T(8,128)S(1)} %get-tuple-element.8.gw_in), custom_call_target="tpu_custom_call" | custom-call | tf_op jit(solution)/shard_map/pallas_call | solution.py:594

commit v8 on v7

--- a/solution.py
+++ b/solution.py
@@ -35,6 +35,8 @@
     start_grads,
     own_grads,
     mate_cp,
+    mate_cot,
+    mate_start,
     mate_passed,
     mate_bar,
     part_d,
@@ -53,10 +55,7 @@
     adj_in,
     fwd,
     fwd_in,
-    sum_a,
     sum_b,
-    part_a,
-    part_b,
     gain_send,
     gain_recv,
     adj_send,
@@ -65,10 +64,6 @@
     fwd_recv,
     edge_send,
     edge_recv,
-    a_send,
-    a_recv,
-    b_send,
-    b_recv,
     c_send,
     c_recv,
 ):
@@ -224,6 +219,14 @@
             cp_ref.at[0, 0], mate_cp, mate_send.at[0], mate_recv.at[0], {"dp": across}
         )
 
+    def mate_cot_copy():
+        return along(
+            cot_ref.at[0, 0], mate_cot, mate_send.at[3], mate_recv.at[3], {"dp": across}
+        )
+
+    def mate_start_copy():
+        return along(start_buf, mate_start, mate_send.at[4], mate_recv.at[4], {"dp": across})
+
     def mate_passed_copy():
         return along(passed_buf, mate_passed, mate_send.at[1], mate_recv.at[1], {"dp": across})
 
@@ -300,6 +303,7 @@
     if rounds > 1:
         start_gain(0)
     mate_cp_copy().start()
+    mate_cot_copy().start()
     for layer in range(1, layers):
         fetches[3 + layer].wait()
         stack(layer)
@@ -350,6 +354,7 @@
     def _():
         start_buf[...] = own
 
+    mate_start_copy().start()
     mate_cp_copy().wait_recv()
     u = start_buf[...]
     v = mate_cp[...]
@@ -365,20 +370,6 @@
     mine = pl.ds(pl.multiple_of(side * half, half), half)
     other = pl.ds(pl.multiple_of((1 - side) * half, half), half)
 
-    def a_copy(layer):
-        return along(
-            start_grads.at[layer, other],
-            part_a.at[layer],
-            a_send.at[layer],
-            a_recv.at[layer],
-            {"dp": sibling},
-        )
-
-    def b_copy(layer):
-        return along(
-            sum_a.at[layer], part_b.at[layer], b_send.at[layer], b_recv.at[layer], {"dp": across}
-        )
-
     def c_copy(layer):
         return along(
             sum_b.at[layer],
@@ -388,11 +379,6 @@
             {"dp": sibling},
         )
 
-    def middle(layer):
-        a_copy(layer).wait_recv()
-        sum_a[layer] = start_grads[layer, mine, :] + part_a[layer]
-        b_copy(layer).start()
-
     def d_copy(layer):
         return along(
             own_grads.at[layer, other],
@@ -403,10 +389,8 @@
         )
 
     def last(layer):
-        b_copy(layer).wait_recv()
-        starts = sum_a[layer] + part_b[layer]
         d_copy(layer).wait_recv()
-        sum_b[layer] = starts + (own_grads[layer, mine, :] + part_d[layer])
+        sum_b[layer] = own_grads[layer, mine, :] + part_d[layer]
         c_copy(layer).start()
         gw_ref[layer, mine, :] = sum_b[layer]
 
@@ -414,9 +398,6 @@
     for position, layer in enumerate(reversed(range(layers))):
         g, grads = backward_layer(g, layer, 1)
         start_grads[layer] = grads
-        a_copy(layer).start()
-        if position == 2:
-            middle(layer + 2)
         if position == layers - 2:
             take_fwd(0)
             if rounds > 1:
@@ -428,12 +409,21 @@
         back_copy().start()
         mate_back_copy().start()
 
-    for layer in reversed(range(layers - 1)):
-        middle(layer)
     for r in range(1, rounds - 1):
         take_fwd(r)
         start_fwd(r + 1)
 
+    mate_start_copy().wait_recv()
+    v = mate_start[...]
+    for layer in range(layers):
+        v = forward_layer(v, layer, 3)
+    mate_cot_copy().wait_recv()
+    mate_passed_copy().wait_recv()
+    h = mate_cot[...] + mate_passed[...]
+    for layer in reversed(range(layers)):
+        h, mate_grads = backward_layer(h, layer, 3)
+        start_grads[layer] = start_grads[layer] + mate_grads
+
     @pl.when(me + 1 < depth)
     def _():
         back_copy().wait_recv()
@@ -444,14 +434,13 @@
         bar_buf[...] = jnp.zeros_like(bar_buf)
         mate_bar[...] = jnp.zeros_like(mate_bar)
 
-    mate_passed_copy().wait_recv()
     g = bar_buf[...] - passed_buf[...]
     h = mate_bar[...] - mate_passed[...]
 
     for layer in reversed(range(layers)):
         g, grads = backward_layer(g, layer, 0)
         h, mate_grads = backward_layer(h, layer, 2)
-        own_grads[layer] = grads + mate_grads
+        own_grads[layer] = start_grads[layer] + (grads + mate_grads)
         d_copy(layer).start()
     gcp_ref[0, 0] = g + jnp.where(me == 0, 1.0, 0.0) * back_buf[...]
     for layer in reversed(range(layers)):
@@ -461,11 +450,11 @@
     corr_ref[0, 0] = fwd[rounds]
     for layer in reversed(range(layers)):
         c_copy(layer).wait_recv()
-        a_copy(layer).wait_send()
-        b_copy(layer).wait_send()
         c_copy(layer).wait_send()
         d_copy(layer).wait_send()
     mate_cp_copy().wait_send()
+    mate_cot_copy().wait_send()
+    mate_start_copy().wait_send()
     mate_passed_copy().wait_send()
 
     for r in range(rounds):
@@ -538,8 +527,8 @@
                 pltpu.VMEM(coarse_gain.shape, f32),
                 pltpu.VMEM(cotangent.shape, f32),
                 dma((3 + layers,)),
-                pltpu.VMEM((3, layers, width // 3, pixels), bf16),
-                pltpu.VMEM((3, layers) + state, f32),
+                pltpu.VMEM((4, layers, width // 3, pixels), bf16),
+                pltpu.VMEM((4, layers) + state, f32),
                 pltpu.VMEM((2, width // 3, pixels), bf16),
                 pltpu.VMEM((2, width // 3, pixels), bf16),
                 pltpu.VMEM((layers, 3 * channels, width // 3), bf16),
@@ -549,9 +538,11 @@
                 pltpu.VMEM(state, f32),
                 pltpu.VMEM(state, f32),
                 pltpu.VMEM(state, f32),
+                pltpu.VMEM(state, f32),
+                pltpu.VMEM(state, f32),
                 pltpu.VMEM(half, f32),
-                dma((3,)),
-                dma((3,)),
+                dma((5,)),
+                dma((5,)),
                 dma((layers,)),
                 dma((layers,)),
                 pltpu.VMEM(state, f32),
@@ -565,9 +556,6 @@
                 pltpu.VMEM((rounds,) + state, f32),
                 pltpu.VMEM((rounds + 1,) + state, f32),
                 pltpu.VMEM((rounds,) + state, f32),
-                pltpu.VMEM(half, f32),
-                pltpu.VMEM(half, f32),
-                pltpu.VMEM(half, f32),
                 pltpu.VMEM(half, f32),
                 dma((rounds,)),
                 dma((rounds,)),
@@ -577,10 +565,6 @@
                 dma((rounds,)),
                 dma((2,)),
                 dma((2,)),
-                dma((layers,)),
-                dma((layers,)),
-                dma((layers,)),
-                dma((layers,)),
                 dma((layers,)),
                 dma((layers,)),
             ],

time: 32 us -> 30 us (0.938)
  Pallas kernels: 31.2 us -> 29.2 us
    pallas_call x1, Pallas kernels: 30.2 us -> 28.2 us  [step(): pl.pallas_call(functools.partial(kernel, depth, dp), out_shape=results, i...]
where the time goes in v8:
time: 30 us; the launch traced here: 29.8 us
  Pallas kernels  29.2 us (97%)
  between operations  0.64 us (2%)
    pallas_call x1, Pallas kernels, step(): pl.pallas_call(functools.partial(kernel, depth, dp), out_shape=results, i...  28.2 us
    pallas_call x1, Pallas kernels, step(): pl.pallas_call(deliver, out_shape=results, in_specs=[vmem] * 3, out_specs...  0.93 us

profile of v8, /device:TPU:0, one launch (start us, length us, event | category | flops | bytes accessed | tf_op | source)
XLA Modules:
  0.0 29.8 jit_solution(17350824489886426657)
XLA Ops:
  0.6 28.2 %shard_map.67 = (f32[1,1,64,256]{3,2,1,0:T(8,128)S(1)}, f32[1,1,64,256]{3,2,1,0:T(8,128)S(1)}, f32[4,64,576]{2,1,0:T(8,128)S(1)}) custom-call(f32[1,1,64,256]{3,2,1,0:T(8,128)} %cp_hbm.1, bf16[4,64,576]{2,1,0:T(8,128)(2,1)} %w_hbm.1, f32[1,64]{1,0:T(1,128)} %gain_hbm.1, f32[1,1,64,256]{3,2,1,0:T(8,128)} %cot_hbm.1), custom_call_target="tpu_custom_call" | custom-call | tf_op jit(solution)/shard_map/pallas_call | solution.py:519
  28.9 0.9 %shard_map.68 = (f32[1,1,64,256]{3,2,1,0:T(8,128)}, f32[1,1,64,256]{3,2,1,0:T(8,128)}, f32[4,64,576]{2,1,0:T(8,128)}) custom-call(f32[1,1,64,256]{3,2,1,0:T(8,128)S(1)} %get-tuple-element.6.corr_in, f32[1,1,64,256]{3,2,1,0:T(8,128)S(1)} %get-tuple-element.7.gcp_in, f32[4,64,576]{2,1,0:T(8,128)S(1)} %get-tuple-element.8.gw_in), custom_call_target="tpu_custom_call" | custom-call | tf_op jit(solution)/shard_map/pallas_call | solution.py:578

commit v9 on v8

--- a/solution.py
+++ b/solution.py
@@ -55,7 +55,6 @@
     adj_in,
     fwd,
     fwd_in,
-    sum_b,
     gain_send,
     gain_recv,
     adj_send,
@@ -64,8 +63,6 @@
     fwd_recv,
     edge_send,
     edge_recv,
-    c_send,
-    c_recv,
 ):
     layers, channels, width = w_ref.shape
     pixels = cp_ref.shape[-1]
@@ -88,8 +85,7 @@
     rounds = len(hops)
     me = lax.axis_index("depth")
     lane = lax.axis_index("dp")
-    side = lane % 2
-    sibling = lane + 1 - 2 * side
+    sibling = lane + 1 - 2 * (lane % 2)
     across = (lane + 2) % dp
 
     barrier = pltpu.get_barrier_semaphore()
@@ -367,21 +363,9 @@
         take_adj(rounds - 1, n)
     mate_passed_copy().start()
 
-    mine = pl.ds(pl.multiple_of(side * half, half), half)
-    other = pl.ds(pl.multiple_of((1 - side) * half, half), half)
-
-    def c_copy(layer):
-        return along(
-            sum_b.at[layer],
-            gw_ref.at[layer, mine],
-            c_send.at[layer],
-            c_recv.at[layer],
-            {"dp": sibling},
-        )
-
     def d_copy(layer):
         return along(
-            own_grads.at[layer, other],
+            own_grads.at[layer],
             part_d.at[layer],
             d_send.at[layer],
             d_recv.at[layer],
@@ -390,9 +374,7 @@
 
     def last(layer):
         d_copy(layer).wait_recv()
-        sum_b[layer] = own_grads[layer, mine, :] + part_d[layer]
-        c_copy(layer).start()
-        gw_ref[layer, mine, :] = sum_b[layer]
+        gw_ref[layer] = own_grads[layer] + part_d[layer]
 
     g = cot_ref[0, 0] + passed_buf[...]
     for position, layer in enumerate(reversed(range(layers))):
@@ -442,15 +424,15 @@
         h, mate_grads = backward_layer(h, layer, 2)
         own_grads[layer] = start_grads[layer] + (grads + mate_grads)
         d_copy(layer).start()
+        if layer + 2 < layers:
+            last(layer + 2)
     gcp_ref[0, 0] = g + jnp.where(me == 0, 1.0, 0.0) * back_buf[...]
-    for layer in reversed(range(layers)):
-        last(layer)
     if rounds > 1:
         take_fwd(rounds - 1)
     corr_ref[0, 0] = fwd[rounds]
+    for layer in reversed(range(min(2, layers))):
+        last(layer)
     for layer in reversed(range(layers)):
-        c_copy(layer).wait_recv()
-        c_copy(layer).wait_send()
         d_copy(layer).wait_send()
     mate_cp_copy().wait_send()
     mate_cot_copy().wait_send()
@@ -506,7 +488,6 @@
         layers, channels, width = weights.shape
         pixels = cpoints.shape[-1]
         state = (channels, pixels)
-        half = (layers, channels // 2, width)
         f32, bf16 = jnp.float32, jnp.bfloat16
         dma = pltpu.SemaphoreType.DMA
         vmem = pl.BlockSpec(memory_space=pltpu.VMEM)
@@ -540,7 +521,7 @@
                 pltpu.VMEM(state, f32),
                 pltpu.VMEM(state, f32),
                 pltpu.VMEM(state, f32),
-                pltpu.VMEM(half, f32),
+                pltpu.VMEM((layers, channels, width), f32),
                 dma((5,)),
                 dma((5,)),
                 dma((layers,)),
@@ -556,7 +537,6 @@
                 pltpu.VMEM((rounds,) + state, f32),
                 pltpu.VMEM((rounds + 1,) + state, f32),
                 pltpu.VMEM((rounds,) + state, f32),
-                pltpu.VMEM(half, f32),
                 dma((rounds,)),
                 dma((rounds,)),
                 dma((rounds, 2)),
@@ -565,8 +545,6 @@
                 dma((rounds,)),
                 dma((2,)),
                 dma((2,)),
-                dma((layers,)),
-                dma((layers,)),
             ],
             compiler_params=pltpu.CompilerParams(
                 collective_id=0, has_side_effects=True, vmem_limit_bytes=40 * 1024 * 1024

time: 30 us -> 29.3 us (0.977)
  Pallas kernels: 29.2 us -> 28.5 us
    pallas_call x1, Pallas kernels: 28.2 us -> 27.6 us  [step(): pl.pallas_call(functools.partial(kernel, depth, dp), out_shape=results, i...]
where the time goes in v9:
time: 29.3 us; the launch traced here: 29.2 us
  Pallas kernels  28.5 us (97%)
  between operations  0.64 us (2%)
    pallas_call x1, Pallas kernels, step(): pl.pallas_call(functools.partial(kernel, depth, dp), out_shape=results, i...  27.6 us
    pallas_call x1, Pallas kernels, step(): pl.pallas_call(deliver, out_shape=results, in_specs=[vmem] * 3, out_specs...  0.93 us

profile of v9, /device:TPU:0, one launch (start us, length us, event | category | flops | bytes accessed | tf_op | source)
XLA Modules:
  0.0 29.2 jit_solution(16277977189045582801)
XLA Ops:
  0.6 27.6 %shard_map.67 = (f32[1,1,64,256]{3,2,1,0:T(8,128)S(1)}, f32[1,1,64,256]{3,2,1,0:T(8,128)S(1)}, f32[4,64,576]{2,1,0:T(8,128)S(1)}) custom-call(f32[1,1,64,256]{3,2,1,0:T(8,128)} %cp_hbm.1, bf16[4,64,576]{2,1,0:T(8,128)(2,1)} %w_hbm.1, f32[1,64]{1,0:T(1,128)} %gain_hbm.1, f32[1,1,64,256]{3,2,1,0:T(8,128)} %cot_hbm.1), custom_call_target="tpu_custom_call" | custom-call | tf_op jit(solution)/shard_map/pallas_call | solution.py:500
  28.2 0.9 %shard_map.68 = (f32[1,1,64,256]{3,2,1,0:T(8,128)}, f32[1,1,64,256]{3,2,1,0:T(8,128)}, f32[4,64,576]{2,1,0:T(8,128)}) custom-call(f32[1,1,64,256]{3,2,1,0:T(8,128)S(1)} %get-tuple-element.6.corr_in, f32[1,1,64,256]{3,2,1,0:T(8,128)S(1)} %get-tuple-element.7.gcp_in, f32[4,64,576]{2,1,0:T(8,128)S(1)} %get-tuple-element.8.gw_in), custom_call_target="tpu_custom_call" | custom-call | tf_op jit(solution)/shard_map/pallas_call | solution.py:556
